TPU v7x, 32 devices: a whole 2x2x4 slice. The times are simulated.
32 devices in a mesh: dp: 8 (over z, y), seq: 4 (over x, core).
Axes of the slice: x: 2, y: 2, z: 4, core: 2. Of those that a mesh axis runs over, the one named last changes fastest.
Arguments:
- inputs: float32 [512, 64, 768], P('seq', 'dp'), may hold values from -6 to 6
- item_counts: int32 [8], P('dp'), may hold values from 4 to 8, as said below
- lengths: int32 [64], P('dp'), may hold values from 32 to 512, as said below
- gain_one: float32 [768], replicated, may hold values from 0.1 to 1.9
- shift_one: float32 [768], replicated, may hold values from -3 to 3
- weight_in: bfloat16 [768, 3072], replicated, may hold values from -0.21875 to 0.21875
- bias_in: float32 [3072], replicated, may hold values from -3 to 3
- weight_out: bfloat16 [3072, 768], replicated, may hold values from -0.15625 to 0.15625
- bias_out: float32 [768], replicated, may hold values from -3 to 3
- gain_two: float32 [768], replicated, may hold values from 0.1 to 1.9
- shift_two: float32 [768], replicated, may hold values from -3 to 3
- cotangent: float32 [512, 64, 768], P('seq', 'dp'), may hold values from -6 to 6
Outputs:
- layer_out: float32 [512, 64, 768], P('seq', 'dp')
- input_grad: float32 [512, 64, 768], P('seq', 'dp')
- gain_one_grad: float32 [768], replicated
- shift_one_grad: float32 [768], replicated
- weight_in_grad: float32 [768, 3072], replicated
- bias_in_grad: float32 [3072], replicated
- weight_out_grad: float32 [3072, 768], replicated
- bias_out_grad: float32 [768], replicated
- gain_two_grad: float32 [768], replicated
- shift_two_grad: float32 [768], replicated
Inputs may be any that keep to these rules, and one draw needn't show every extreme that they name: `item_counts`: at least one index of dp has all 8 slots in use. `lengths`: slots at or beyond their device's count are empty whatever their length. On every index of dp one slot in use has length 512.
All inputs are finite; a program needn't handle non-finite values.
Results may differ from a plain program's by a relative error of at most 0.0075.
Values may be sent and summed in bfloat16 or wider, within the bound.
A program may use at most 192 MiB of HBM per device.

v0:
```python
import math

import jax
import jax.numpy as jnp
from jax import lax
from jax.sharding import PartitionSpec as P

EPSILON = 1e-05


def dft_tables(count):
    index = jnp.arange(count, dtype=jnp.int32)
    angle = (index[:, None] * index[None, :] % count).astype(jnp.float32) * (2.0 * math.pi / count)
    return (jnp.cos(angle).astype(jnp.bfloat16), jnp.sin(angle).astype(jnp.bfloat16))


def normalize(values):
    center = values - jnp.mean(values, axis=-1, keepdims=True)
    spread = jnp.mean(center * center, axis=-1, keepdims=True)
    inverse = lax.rsqrt(spread + EPSILON)
    return (center * inverse, inverse)


def norm_back(grad_hat, normal, inverse):
    first = jnp.mean(grad_hat, axis=-1, keepdims=True)
    second = jnp.mean(grad_hat * normal, axis=-1, keepdims=True)
    return inverse * (grad_hat - first - normal * second)


def smooth_gate(values):
    return jax.nn.gelu(values, approximate=False)


def contract_rows(left, right):
    return lax.dot_general(
        left, right, (((0,), (0,)), ((), ())), preferred_element_type=jnp.float32
    )


def contract_cols(left, right):
    return lax.dot_general(
        left, right, (((1,), (1,)), ((), ())), preferred_element_type=jnp.float32
    )


def spectral(rounded, tables, again):
    hidden_cos, hidden_sin, seq_cos, seq_sin, dft_scale = tables
    row_count, item_count, features = rounded.shape
    flat = rounded.reshape(row_count * item_count, features)
    cos_part = (
        jnp.dot(flat, hidden_cos, preferred_element_type=jnp.float32)
        .astype(jnp.bfloat16)
        .reshape(row_count, item_count, features)
    )
    sin_part = (
        jnp.dot(flat, hidden_sin, preferred_element_type=jnp.float32)
        .astype(jnp.bfloat16)
        .reshape(row_count, item_count, features)
    )

    def transform(parts):
        cos_cols, sin_cols = parts
        seq_total = cos_cols.shape[0]
        joined = jnp.dot(
            seq_cos, cos_cols.reshape(seq_total, -1), preferred_element_type=jnp.float32
        )
        joined = joined - jnp.dot(
            seq_sin, sin_cols.reshape(seq_total, -1), preferred_element_type=jnp.float32
        )
        return (joined * dft_scale).astype(jnp.bfloat16).reshape(cos_cols.shape)

    if again:
        columns = transform(
            (
                lax.all_to_all(cos_part, "seq", split_axis=2, concat_axis=0, tiled=True),
                lax.all_to_all(sin_part, "seq", split_axis=2, concat_axis=0, tiled=True),
            )
        )
        mixed = lax.all_to_all(columns, "seq", split_axis=0, concat_axis=2, tiled=True)
    else:
        columns = transform(
            (
                lax.all_to_all(cos_part, "seq", split_axis=2, concat_axis=0, tiled=True),
                lax.all_to_all(sin_part, "seq", split_axis=2, concat_axis=0, tiled=True),
            )
        )
        mixed = lax.all_to_all(columns, "seq", split_axis=0, concat_axis=2, tiled=True)
    return mixed.astype(jnp.float32)


def dense_forward(masked_input, mixed, params):
    gain_one, shift_one, weight_in, bias_in, weight_out, bias_out = params
    features = masked_input.shape[2]
    summed = masked_input + mixed
    hat_one, inverse_one = normalize(summed)
    normed = (hat_one * gain_one + shift_one).astype(jnp.bfloat16).reshape(-1, features)
    hidden = jnp.dot(normed, weight_in, preferred_element_type=jnp.float32) + bias_in
    active = smooth_gate(hidden).astype(jnp.bfloat16)
    branch = jnp.dot(active, weight_out, preferred_element_type=jnp.float32) + bias_out
    second = summed + branch.reshape(summed.shape)
    hat_two, inverse_two = normalize(second)
    return (summed, hat_one, inverse_one, normed, hidden, active, hat_two, inverse_two)


def per_device(
    inputs,
    item_counts,
    lengths,
    gain_one,
    shift_one,
    weight_in,
    bias_in,
    weight_out,
    bias_out,
    gain_two,
    shift_two,
    cotangent,
):
    row_count, item_count, features = inputs.shape
    seq_total = row_count * lax.axis_size("seq")
    hidden_cos, hidden_sin = dft_tables(features)
    seq_cos, seq_sin = dft_tables(seq_total)
    tables = (hidden_cos, hidden_sin, seq_cos, seq_sin, 1.0 / math.sqrt(features * seq_total))
    positions = lax.axis_index("seq") * row_count + jnp.arange(row_count, dtype=jnp.int32)
    used_slot = jnp.arange(item_count, dtype=jnp.int32) < item_counts[0]
    live_mask = ((positions[:, None] < lengths[None, :]) & used_slot[None, :]).astype(jnp.float32)[
        :, :, None
    ]
    masked_input = inputs * live_mask
    rounded = masked_input.astype(jnp.bfloat16)
    params = (gain_one, shift_one, weight_in, bias_in, weight_out, bias_out)
    mixed = spectral(rounded, tables, False)
    summed, hat_one, inverse_one, normed, hidden, active, hat_two, inverse_two = dense_forward(
        masked_input, mixed, params
    )
    layer_out = (hat_two * gain_two + shift_two) * live_mask
    mixed_again = spectral(rounded, tables, True)
    summed, hat_one, inverse_one, normed, hidden, active, hat_two, inverse_two = dense_forward(
        masked_input, mixed_again, params
    )
    grad_out = cotangent * live_mask
    grad_gain_two = jnp.sum(grad_out * hat_two, axis=(0, 1))
    grad_shift_two = jnp.sum(grad_out, axis=(0, 1))
    grad_second = norm_back(grad_out * gain_two, hat_two, inverse_two)
    grad_branch = grad_second.astype(jnp.bfloat16).reshape(-1, features)
    grad_bias_out = jnp.sum(grad_branch.astype(jnp.float32), axis=0)
    grad_weight_out = contract_rows(active, grad_branch)
    grad_active = contract_cols(grad_branch, weight_out)
    gate_pull = jax.vjp(smooth_gate, hidden)[1]
    grad_hidden = gate_pull(grad_active)[0].astype(jnp.bfloat16)
    grad_bias_in = jnp.sum(grad_hidden.astype(jnp.float32), axis=0)
    grad_weight_in = contract_rows(normed, grad_hidden)
    grad_normed = contract_cols(grad_hidden, weight_in).reshape(summed.shape)
    grad_gain_one = jnp.sum(grad_normed * hat_one, axis=(0, 1))
    grad_shift_one = jnp.sum(grad_normed, axis=(0, 1))
    grad_summed = grad_second + norm_back(grad_normed * gain_one, hat_one, inverse_one)
    grad_mixed = grad_summed.astype(jnp.bfloat16)
    dft_scale = tables[4]
    piece = lax.all_to_all(grad_mixed, "seq", split_axis=2, concat_axis=0, tiled=True)
    flat_piece = piece.reshape(piece.shape[0], -1)
    grad_cos = (
        jnp.dot(seq_cos, flat_piece, preferred_element_type=jnp.float32) * dft_scale
    ).astype(jnp.bfloat16)
    grad_sin = (
        -(jnp.dot(seq_sin, flat_piece, preferred_element_type=jnp.float32) * dft_scale)
    ).astype(jnp.bfloat16)
    grad_cos_rows, grad_sin_rows = (
        lax.all_to_all(
            grad_cos.reshape(piece.shape), "seq", split_axis=0, concat_axis=2, tiled=True
        ),
        lax.all_to_all(
            grad_sin.reshape(piece.shape), "seq", split_axis=0, concat_axis=2, tiled=True
        ),
    )
    grad_rounded = jnp.dot(
        grad_cos_rows.reshape(-1, features), hidden_cos, preferred_element_type=jnp.float32
    )
    grad_rounded = grad_rounded + jnp.dot(
        grad_sin_rows.reshape(-1, features), hidden_sin, preferred_element_type=jnp.float32
    )
    input_grad = (grad_summed + grad_rounded.reshape(summed.shape)) * live_mask
    shares = (
        lax.psum_scatter(grad_gain_one, ("dp", "seq"), scatter_dimension=0, tiled=True),
        lax.psum_scatter(grad_shift_one, ("dp", "seq"), scatter_dimension=0, tiled=True),
        lax.psum_scatter(grad_weight_in, ("dp", "seq"), scatter_dimension=0, tiled=True),
        lax.psum_scatter(grad_bias_in, ("dp", "seq"), scatter_dimension=0, tiled=True),
        lax.psum_scatter(grad_weight_out, ("dp", "seq"), scatter_dimension=0, tiled=True),
        lax.psum_scatter(grad_bias_out, ("dp", "seq"), scatter_dimension=0, tiled=True),
        lax.psum_scatter(grad_gain_two, ("dp", "seq"), scatter_dimension=0, tiled=True),
        lax.psum_scatter(grad_shift_two, ("dp", "seq"), scatter_dimension=0, tiled=True),
    )
    totals = (
        lax.all_gather(shares[0].astype(jnp.bfloat16), ("dp", "seq"), axis=0, tiled=True).astype(
            jnp.float32
        ),
        lax.all_gather(shares[1].astype(jnp.bfloat16), ("dp", "seq"), axis=0, tiled=True).astype(
            jnp.float32
        ),
        lax.all_gather(shares[2].astype(jnp.bfloat16), ("dp", "seq"), axis=0, tiled=True).astype(
            jnp.float32
        ),
        lax.all_gather(shares[3].astype(jnp.bfloat16), ("dp", "seq"), axis=0, tiled=True).astype(
            jnp.float32
        ),
        lax.all_gather(shares[4].astype(jnp.bfloat16), ("dp", "seq"), axis=0, tiled=True).astype(
            jnp.float32
        ),
        lax.all_gather(shares[5].astype(jnp.bfloat16), ("dp", "seq"), axis=0, tiled=True).astype(
            jnp.float32
        ),
        lax.all_gather(shares[6].astype(jnp.bfloat16), ("dp", "seq"), axis=0, tiled=True).astype(
            jnp.float32
        ),
        lax.all_gather(shares[7].astype(jnp.bfloat16), ("dp", "seq"), axis=0, tiled=True).astype(
            jnp.float32
        ),
    )
    return (
        layer_out,
        input_grad,
        totals[0],
        totals[1],
        totals[2],
        totals[3],
        totals[4],
        totals[5],
        totals[6],
        totals[7],
    )


def solution(mesh):
    placed = (
        P("seq", "dp", None),
        P("dp"),
        P("dp"),
        P(),
        P(),
        P(),
        P(),
        P(),
        P(),
        P(),
        P(),
        P("seq", "dp", None),
    )
    return jax.shard_map(
        per_device,
        mesh=mesh,
        in_specs=placed,
        out_specs=(
            P("seq", "dp", None),
            P("seq", "dp", None),
            P(),
            P(),
            P(),
            P(),
            P(),
            P(),
            P(),
            P(),
        ),
        check_vma=False,
    )
```

profile of v0, /device:TPU:0, one launch (start us, length us, event | category | flops | bytes accessed | tf_op | source)
XLA Modules:
  0.0 750.8 jit_solution(6384576616352926924)
XLA Ops:
  8.7 11.5 %fusion.30 = bf16[128,8,768]{2,1,0:T(8,128)(2,1)S(1)} fusion(f32[128,8,768]{2,1,0:T(8,128)} %param.12, f32[128,8]{1,0:T(8,128)S(1)} %copy.114), kind=kOutput, calls=%fused_computation.77 | convolution fusion | flops 1216217088 | bytes 4722688 | tf_op jit(solution)/shard_map/dot_general | solution.py:51
  22.5 4.4 all-to-all-start
  26.9 11.5 %fusion.31 = bf16[128,8,768]{2,1,0:T(8,128)(2,1)S(1)} fusion(f32[128,8,768]{2,1,0:T(8,128)} %param.12, f32[128,8]{1,0:T(8,128)S(1)} %copy.114), kind=kOutput, calls=%fused_computation.78 | convolution fusion | flops 1216217088 | bytes 4722688 | tf_op jit(solution)/shard_map/dot_general | solution.py:56
  40.7 6.2 all-to-all-done
  52.0 6.0 fusion.24
  58.0 12.5 %all-to-all-done.1 = bf16[128,8,768]{0,1,2:T(8,128)(2,1)S(1)} async-done(((bf16[128,8,768]{0,1,2:T(8,128)(2,1)}), bf16[128,8,768]{0,1,2:T(8,128)(2,1)S(1)}, u32[]{:S(2)}, u32[]{:S(2)}) %all-to-all-start.1) | async-done | bytes 1572896 | tf_op jit(solution)/shard_map/all_to_all | solution.py:84
  72.4 4.9 fusion.11
  82.2 29.3 %all_to_all.99 = bf16[512,8,192]{2,1,0:T(8,128)(2,1)} all-to-all(bf16[512,8,192]{2,1,0:T(8,128)(2,1)S(1)} %copy.122), channel_id=1, replica_groups=mesh['dp'=8,'seq'=4] {'seq'}, dimensions={0} | all-to-all | bytes 3145728 | tf_op jit(solution)/shard_map/all_to_all | solution.py:87
  111.5 4.4 copy.123
  128.6 37.3 %multiply_convert_fusion = (bf16[1024,3072]{1,0:T(8,128)(2,1)S(1)}, f32[1024,3072]{1,0:T(8,128)}, f32[1024,3072]{1,0:T(8,128)}) fusion(f32[3072]{0:T(1024)S(1)} %copy-done.10, bf16[768,3072]{1,0:T(8,128)(2,1)} %param.17, f32[128,8,768]{2,1,0:T(8,128)S(1)} %get-tuple-element.47, f32[768]{0:T(1024)S(1)} %copy-done.7, f32[768]{0:T(1024)S(1)} %copy-done.6, ...), kind=kOutput, calls=%fused_computation.4 | convolution fusion | flops 5043388416 | bytes 39348224 | tf_op jit(solution)/shard_map/dot_general | solution.py:97
  166.0 5.3 fusion.81
  178.6 18.7 %convert_reduce_fusion = (f32[3072]{0:T(1024)S(1)}, bf16[1024,3072]{1,0:T(8,128)(2,1)}) fusion(f32[1024,3072]{1,0:T(8,128)} %get-tuple-element.45, bf16[3072,768]{1,0:T(8,128)(2,1)} %param.19, f32[128,8,768]{2,1,0:T(8,128)} %get-tuple-element.41, f32[1024,3072]{1,0:T(8,128)} %get-tuple-element.49, f32[3072]{0:T(1024)S(1)} %copy-done.10), kind=kOutput, calls=%fused_computation.2 | convolution fusion | flops 4886098944 | bytes 39346176 | tf_op jit(solution)/shard_map/dot_general | solution.py:41
  197.2 10.9 %fusion.73 = f32[768,3072]{1,0:T(8,128)} fusion(bf16[1024,3072]{1,0:T(8,128)(2,1)} %get-tuple-element.54, f32[128,8,768]{2,1,0:T(8,128)S(1)} %get-tuple-element.47, f32[768]{0:T(1024)S(1)} %copy-done.7, f32[768]{0:T(1024)S(1)} %copy-done.6, f32[128,8]{1,0:T(8,128)S(1)} %add_rsqrt_fusion.1, f32[128,8]{1,0:T(8,128)S(1)} %broadcast_multiply_fusion.4), kind=kOutput, calls=%fused_computation.137 | convolution fusion | flops 4835770368 | bytes 18888704 | tf_op jit(solution)/shard_map/dot_general | solution.py:35
  208.2 10.4 %fusion.27 = f32[3072,768]{1,0:T(8,128)} fusion(bf16[1024,3072]{1,0:T(8,128)(2,1)} %copy-done.13, f32[128,8,768]{2,1,0:T(8,128)} %get-tuple-element.41), kind=kOutput, calls=%fused_computation.71 | convolution fusion | flops 4832624640 | bytes 18874368 | tf_op jit(solution)/shard_map/dot_general | solution.py:35
  218.7 126.3 %reduce-scatter.3.cloned.1.call-done = f32[24,3072]{1,0:T(8,128)} async-done(((f32[768,3072]{1,0:T(8,128)}), f32[24,3072]{1,0:T(8,128)}) %reduce-scatter.3.cloned.1.call-update) | async-done | bytes 294928 | tf_op jit(solution)/shard_map/reduce_scatter | solution.py:185
  346.7 140.3 %reduce-scatter.5.cloned.1.call-done = f32[96,768]{1,0:T(8,128)} async-done(((f32[3072,768]{1,0:T(8,128)}), f32[96,768]{1,0:T(8,128)}) %reduce-scatter.5.cloned.1.call-update) | async-done | bytes 294928 | tf_op jit(solution)/shard_map/reduce_scatter | solution.py:187
  488.7 9.0 %fusion.9 = (f32[768]{0:T(1024)S(1)}, f32[128,8]{1,0:T(8,128)S(1)}, f32[1024,768]{1,0:T(8,128)S(1)}) fusion(f32[128,8,768]{2,1,0:T(8,128)S(1)} %get-tuple-element.47, f32[128,8]{1,0:T(8,128)S(1)} %add_rsqrt_fusion.1, f32[128,8]{1,0:T(8,128)S(1)} %broadcast_multiply_fusion.4, f32[768]{0:T(1024)S(1)} %copy-done.6, bf16[1024,3072]{1,0:T(8,128)(2,1)} %get-tuple-element.54, ...), kind=kOutput, calls=%fused_computation.28 | convolution fusion | flops 4837341184 | bytes 17319936 | tf_op jit(solution)/shard_map/dot_general | solution.py:41
  499.9 4.8 fusion.78
  507.1 27.2 %all_to_all.100 = bf16[128,8,768]{0,1,2:T(8,128)(2,1)S(1)} all-to-all(bf16[128,8,768]{0,1,2:T(8,128)(2,1)S(1)} %copy.126), channel_id=1, replica_groups=mesh['dp'=8,'seq'=4] {'seq'}, dimensions={2} | all-to-all | bytes 3145728 | tf_op jit(solution)/shard_map/all_to_all | solution.py:159
  536.7 4.9 fusion.12
  549.0 7.3 fusion.10
  558.9 4.4 copy.133
  563.3 12.5 %all-to-all-done.4 = bf16[512,8,192]{2,1,0:T(8,128)(2,1)S(1)} async-done(((bf16[512,8,192]{2,1,0:T(8,128)(2,1)}), bf16[512,8,192]{2,1,0:T(8,128)(2,1)S(1)}, u32[]{:S(2)}, u32[]{:S(2)}) %all-to-all-start.4) | async-done | bytes 1572896 | tf_op jit(solution)/shard_map/all_to_all | solution.py:168
  575.7 4.4 all-to-all-start.5
  580.2 66.5 %all-reduce.12 = (bf16[768]{0:T(1024)(128)(2,1)S(1)}, bf16[768]{0:T(1024)(128)(2,1)S(1)}, bf16[3072]{0:T(1024)(128)(2,1)S(1)}, bf16[768]{0:T(1024)(128)(2,1)S(1)...) all-reduce(f32[768]{0:T(1024)S(1)} %get-tuple-element.22, ...), channel_id=2, replica_groups=mesh['dp'=8,'seq'=4] {'dp','seq'}, use_global_device_ids=true, to_apply=%region_9.10.clone | all-reduce | flops 6912 | bytes 41472
  648.4 40.2 %all-reduce.13 = (bf16[768]{0:T(1024)(128)(2,1)S(1)}, bf16[768]{0:T(1024)(128)(2,1)S(1)}, bf16[3072]{0:T(1024)(128)(2,1)S(1)}, bf16[768]{0:T(1024)(128)(2,1)S(1)...) all-reduce(bf16[768]{0:T(1024)(128)(2,1)S(1)} %dynamic-update-slice, ...), channel_id=1, replica_groups=mesh['dp'=8,'seq'=4] {'dp','seq'}, use_global_device_ids=true, to_apply=%add | all-reduce | flops 6912 | bytes 27648
  692.2 4.3 copy.160
  699.3 4.3 copy.159
  706.6 11.2 %fusion.34 = f32[1024,768]{1,0:T(8,128)S(1)} fusion(bf16[1024,768]{1,0:T(8,128)(2,1)} %reshape.197), kind=kOutput, calls=%fused_computation.81 | convolution fusion | flops 1213857792 | bytes 4718592 | tf_op jit(solution)/shard_map/dot_general | solution.py:175
  717.9 11.8 %fusion.8 = f32[128,8,768]{2,1,0:T(8,128)} fusion(f32[128,8,768]{2,1,0:T(8,128)S(1)} %copy-done.3, f32[1024,768]{1,0:T(8,128)S(1)} %fusion.34, bf16[1024,768]{1,0:T(8,128)(2,1)S(1)} %copy-done.4, f32[128,8]{1,0:T(8,128)S(1)} %copy.114), kind=kOutput, calls=%fused_computation.25 | convolution fusion | flops 1216217088 | bytes 11014144 | tf_op jit(solution)/shard_map/dot_general | solution.py:178
  729.7 7.4 convert_element_type.178
  737.0 6.8 convert_element_type.183
  (106 shorter events, 68.5 us)
Async XLA Ops:
  22.5 24.4 %all-to-all-start = ((bf16[128,8,768]{0,1,2:T(8,128)(2,1)}), bf16[128,8,768]{0,1,2:T(8,128)(2,1)S(1)}, u32[]{:S(2)}, u32[]{:S(2)}) async-start(bf16[128,8,768]{0,1,2:T(8,128)(2,1)} %copy.115), calls=%async_computation | async-start | bytes 3145728 | tf_op jit(solution)/shard_map/all_to_all | solution.py:83
  46.9 23.6 %all-to-all-start.1 = ((bf16[128,8,768]{0,1,2:T(8,128)(2,1)}), bf16[128,8,768]{0,1,2:T(8,128)(2,1)S(1)}, u32[]{:S(2)}, u32[]{:S(2)}) async-start(bf16[128,8,768]{0,1,2:T(8,128)(2,1)} %copy.118), calls=%async_computation.1 | async-start | bytes 3145728 | tf_op jit(solution)/shard_map/all_to_all | solution.py:84
  50.5 294.5 %reduce-scatter.3.cloned.1.call-start = ((), (), s32[]{:S(2)}) async-start(), calls=%async_computation.8 | async-start | bytes 9732096 | tf_op jit(solution)/shard_map/reduce_scatter | solution.py:185
  70.5 1.9 copy-start.12
  124.4 41.6 %slice-start = ((s8[4718592]{0:T(1024)(128)(4,1)}), s8[4194304]{0:T(1024)(128)(4,1)S(1)}, s32[]{:S(2)}) async-start(s8[4718592]{0:T(1024)(128)(4,1)} %bitcast.111), calls=%async_computation.12 | async-start | bytes 8388608
  127.9 0.7 copy-start.6
  127.9 0.7 copy-start.7
  127.9 0.7 copy-start.10
  128.6 37.3 %slice-start.1 = ((s8[4718592]{0:T(1024)(128)(4,1)}), s8[524288]{0:T(1024)(128)(4,1)S(1)}, s32[]{:S(2)}) async-start(s8[4718592]{0:T(1024)(128)(4,1)} %bitcast.111), calls=%async_computation.13 | async-start | bytes 1048576
  128.6 37.3 %copy-start.11 = (f32[768]{0:T(1024)S(1)}, f32[768]{0:T(1024)}, u32[]{:S(2)}) copy-start(f32[768]{0:T(1024)} %param.20) | copy-start | bytes 9220
  166.0 5.3 copy-start.13
  171.3 1.9 copy-start
  171.3 1.9 copy-start.8
  173.2 1.9 copy-start.9
  208.1 278.9 %reduce-scatter.5.cloned.1.call-start = ((), (), s32[]{:S(2)}) async-start(), calls=%async_computation.10 | async-start | bytes 9732096 | tf_op jit(solution)/shard_map/reduce_scatter | solution.py:187
  218.6 511.1 %all-gather.3.cloned.1.call-start = ((), (), s32[]{:S(2)}) async-start(), calls=%async_computation.9 | async-start | bytes 4866048 | tf_op jit(solution)/shard_map/all_gather | solution.py:199
  346.7 390.4 %all-gather.5.cloned.1.call-start = ((), (), s32[]{:S(2)}) async-start(), calls=%async_computation.11 | async-start | bytes 4866048 | tf_op jit(solution)/shard_map/all_gather | solution.py:205
  497.7 1.7 copy-start.1
  535.6 1.1 copy-start.5
  545.4 30.4 %all-to-all-start.4 = ((bf16[512,8,192]{2,1,0:T(8,128)(2,1)}), bf16[512,8,192]{2,1,0:T(8,128)(2,1)S(1)}, u32[]{:S(2)}, u32[]{:S(2)}) async-start(bf16[512,8,192]{2,1,0:T(8,128)(2,1)} %copy.130), calls=%async_computation.4 | async-start | bytes 4194304 | tf_op jit(solution)/shard_map/all_to_all | solution.py:168
  575.7 116.4 %copy-start.2 = (bf16[512,8,192]{2,1,0:T(8,128)(2,1)}, bf16[512,8,192]{2,1,0:T(8,128)(2,1)S(1)}, u32[]{:S(2)}) copy-start(bf16[512,8,192]{2,1,0:T(8,128)(2,1)S(1)} %all-to-all-done.4) | copy-start | bytes 4718596
  575.7 123.6 %all-to-all-start.5 = ((bf16[512,8,192]{2,1,0:T(8,128)(2,1)}), bf16[512,8,192]{2,1,0:T(8,128)(2,1)}, u32[]{:S(2)}, u32[]{:S(2)}) async-start(bf16[512,8,192]{2,1,0:T(8,128)(2,1)} %copy.133), calls=%async_computation.5 | async-start | bytes 4194304 | tf_op jit(solution)/shard_map/all_to_all | solution.py:171
  706.6 11.3 %copy-start.3 = (f32[128,8,768]{2,1,0:T(8,128)S(1)}, f32[128,8,768]{2,1,0:T(8,128)}, u32[]{:S(2)}) copy-start(f32[128,8,768]{2,1,0:T(8,128)} %get-tuple-element.43) | copy-start | bytes 9437188
  706.6 11.3 %copy-start.4 = (bf16[1024,768]{1,0:T(8,128)(2,1)S(1)}, bf16[1024,768]{1,0:T(8,128)(2,1)}, u32[]{:S(2)}) copy-start(bf16[1024,768]{1,0:T(8,128)(2,1)} %reshape.199) | copy-start | bytes 4718596
Sparse Core Ops, SparseCore 0:
  208.2 136.7 reduce-scatter.2
  352.5 134.5 reduce-scatter.4
  490.0 65.5 all-gather.2
  558.3 69.6 all-gather.4
where the time goes:
time: 760 us; the launch traced here: 751 us
  waiting for transfers between devices  298 us (39%)
  blocking collectives  163 us (21%)
  matrix products  161 us (21%)
  local copies, waits for them, and re-layouts  60.4 us (8%)
  other arithmetic  36.8 us (5%)
  starting transfers between devices  16.4 us (2%)
  between operations  15.3 us (2%)
    reduce_scatter x1, waiting for transfers between devices, per_device(): lax.psum_scatter(grad_weight_out, ('dp', 'seq'), scatter_dimension=0, til...  140 us
    reduce_scatter x1, waiting for transfers between devices, per_device(): lax.psum_scatter(grad_weight_in, ('dp', 'seq'), scatter_dimension=0, tile...  126 us
    unnamed x2, blocking collectives  107 us
    dot_general x1, matrix products, dense_forward(): jnp.dot(normed, weight_in, preferred_element_type=jnp.float32) + bias_in  37.3 us
    all_to_all x1, blocking collectives, spectral(): lax.all_to_all(columns, 'seq', split_axis=0, concat_axis=2, tiled=True)  29.3 us
    dot_general x2, matrix products, contract_cols(): lax.dot_general(left, right, (((1,), (1,)), ((), ())), preferred_element_...  27.7 us
    all_to_all x1, blocking collectives, per_device(): lax.all_to_all(grad_mixed, 'seq', split_axis=2, concat_axis=0, tiled=True)  27.2 us
    dot_general x2, matrix products, contract_rows(): lax.dot_general(left, right, (((0,), (0,)), ((), ())), preferred_element_...  21.3 us
  transfers between devices with their start and end apart: 8, of which 5 were waited for; matrix products, arithmetic and copies ran while one was open for 17% of the time, Pallas kernels for 0%

commit v1 on v0

--- a/solution.py
+++ b/solution.py
@@ -1,11 +1,121 @@
+import functools
 import math
 
 import jax
 import jax.numpy as jnp
 from jax import lax
+from jax.experimental import pallas as pl
+from jax.experimental.pallas import tpu as pltpu
 from jax.sharding import PartitionSpec as P
 
 EPSILON = 1e-05
+MESH = pl.DeviceIdType.MESH
+
+def cube_bits(sizes):
+    bits = []
+    for axis, name in ((1, "seq"), (0, "dp")):
+        k = 1
+        while k < sizes[name]:
+            bits.append((axis, k)); k *= 2
+    return bits
+
+def orders_of(bits):
+    first, rest = bits[:1], bits[1:]
+    return [first + rest, first + [rest[1], rest[0]] + rest[2:], first + [rest[2], rest[0], rest[1]] + rest[3:]]
+
+class Cube:
+    def __init__(self, sizes):
+        self.me = (lax.axis_index("dp"), lax.axis_index("seq"))
+        self.orders = orders_of(cube_bits(sizes))
+        self.stages = len(self.orders[0])
+    def value(self, bit):
+        axis, k = bit
+        return (self.me[axis] // k) % 2
+    def partner(self, bit):
+        axis, k = bit
+        other = self.me[axis] + k * (1 - 2 * self.value(bit))
+        return (other, self.me[1]) if axis == 0 else (self.me[0], other)
+    def offset(self, order, level, rows):
+        off = 0
+        for s in range(level):
+            off = off + self.value(self.orders[order][s]) * (rows >> (s + 1))
+        return off
+
+def ar_kernel(sizes, lags, x_ref, o_ref, buf, full, *rest):
+    n_chunk, rows, _ = buf.shape
+    cube = Cube(sizes)
+    S = cube.stages
+    recv = rest[:S]
+    insem, outsem, rs_s, rs_r, ag_s, ag_r = rest[S:]
+    bar = pltpu.get_barrier_semaphore()
+    for bit in cube.orders[0]:
+        pl.semaphore_signal(bar, inc=1, device_id=cube.partner(bit), device_id_type=MESH)
+    pl.semaphore_wait(bar, S)
+    def load(c): return pltpu.make_async_copy(x_ref.at[c], buf.at[c], insem.at[c])
+    def out(c): return pltpu.make_async_copy(full.at[c], o_ref.at[c], outsem.at[c])
+    def rs(c, o, s):
+        bit = cube.orders[o][s]; h = rows >> (s + 1)
+        off = cube.offset(o, s, rows) + (1 - cube.value(bit)) * h
+        return pltpu.make_async_remote_copy(src_ref=buf.at[c, pl.ds(pl.multiple_of(off, 16), h)], dst_ref=recv[s].at[c],
+            send_sem=rs_s.at[s, c], recv_sem=rs_r.at[s, c], device_id=cube.partner(bit), device_id_type=MESH)
+    def ag(c, o, s):
+        bit = cube.orders[o][s]; h = rows >> (s + 1)
+        off = pl.multiple_of(cube.offset(o, s + 1, rows), 16)
+        return pltpu.make_async_remote_copy(src_ref=full.at[c, pl.ds(off, h)], dst_ref=full.at[c, pl.ds(off, h)],
+            send_sem=ag_s.at[s, c], recv_sem=ag_r.at[s, c], device_id=cube.partner(bit), device_id_type=MESH)
+    def add(c, o, s):
+        h = rows >> (s + 1)
+        off = pl.multiple_of(cube.offset(o, s + 1, rows), 16)
+        target = full if s == S - 1 else buf
+        target[c, pl.ds(off, h), :] = (buf[c, pl.ds(off, h), :].astype(jnp.float32) + recv[s][c].astype(jnp.float32)).astype(jnp.bfloat16)
+    def event(k, c, o):
+        if k == 0:
+            load(c).wait()
+            rs(c, o, 0).start()
+        elif k < S:
+            rs(c, o, k - 1).wait()
+            add(c, o, k - 1)
+            rs(c, o, k).start()
+        elif k == S:
+            rs(c, o, S - 1).wait()
+            add(c, o, S - 1)
+            ag(c, o, S - 1).start()
+        elif k < 2 * S:
+            s = 2 * S - k
+            ag(c, o, s).wait()
+            ag(c, o, s - 1).start()
+        else:
+            ag(c, o, 0).wait()
+            out(c).start()
+    def pre(c, _):
+        load(c).start(); return 0
+    lax.fori_loop(0, n_chunk, pre, 0)
+    when = [0]
+    for l in lags: when.append(when[-1] + l)
+    total = n_chunk + when[-1]
+    def body(g, _):
+        for j in range(3):
+            for k in reversed(range(2 * S + 1)):
+                c = 3 * g + j - when[k]
+                o = (j - when[k]) % 3
+                @pl.when((c >= 0) & (c < n_chunk))
+                def _(): event(k, c, o)
+        return 0
+    lax.fori_loop(0, -(-total // 3), body, 0)
+    def post(c, _):
+        out(c).wait(); return 0
+    lax.fori_loop(0, n_chunk, post, 0)
+
+def all_reduce(x, sizes, lags, cid, name="ar"):
+    n_chunk, rows, lanes = x.shape
+    S = len(cube_bits(sizes))
+    lags = (lags[: S] + [2] * S)[: S] + ([2] * S + lags[-S:])[-S:]
+    return pl.pallas_call(functools.partial(ar_kernel, sizes, lags), name=name,
+        out_shape=jax.ShapeDtypeStruct(x.shape, x.dtype),
+        in_specs=[pl.BlockSpec(memory_space=pl.ANY)], out_specs=pl.BlockSpec(memory_space=pl.ANY),
+        scratch_shapes=[pltpu.VMEM(x.shape, x.dtype)] * 2 + [pltpu.VMEM((n_chunk, rows >> (s + 1), lanes), x.dtype) for s in range(S)]
+          + [pltpu.SemaphoreType.DMA((n_chunk,))] * 2 + [pltpu.SemaphoreType.DMA((S, n_chunk))] * 4,
+        compiler_params=pltpu.CompilerParams(collective_id=cid, has_side_effects=True, vmem_limit_bytes=58 << 20))(x)
 
 
 def dft_tables(count):
@@ -179,53 +289,38 @@
         grad_sin_rows.reshape(-1, features), hidden_sin, preferred_element_type=jnp.float32
     )
     input_grad = (grad_summed + grad_rounded.reshape(summed.shape)) * live_mask
-    shares = (
-        lax.psum_scatter(grad_gain_one, ("dp", "seq"), scatter_dimension=0, tiled=True),
-        lax.psum_scatter(grad_shift_one, ("dp", "seq"), scatter_dimension=0, tiled=True),
-        lax.psum_scatter(grad_weight_in, ("dp", "seq"), scatter_dimension=0, tiled=True),
-        lax.psum_scatter(grad_bias_in, ("dp", "seq"), scatter_dimension=0, tiled=True),
-        lax.psum_scatter(grad_weight_out, ("dp", "seq"), scatter_dimension=0, tiled=True),
-        lax.psum_scatter(grad_bias_out, ("dp", "seq"), scatter_dimension=0, tiled=True),
-        lax.psum_scatter(grad_gain_two, ("dp", "seq"), scatter_dimension=0, tiled=True),
-        lax.psum_scatter(grad_shift_two, ("dp", "seq"), scatter_dimension=0, tiled=True),
-    )
-    totals = (
-        lax.all_gather(shares[0].astype(jnp.bfloat16), ("dp", "seq"), axis=0, tiled=True).astype(
-            jnp.float32
-        ),
-        lax.all_gather(shares[1].astype(jnp.bfloat16), ("dp", "seq"), axis=0, tiled=True).astype(
-            jnp.float32
-        ),
-        lax.all_gather(shares[2].astype(jnp.bfloat16), ("dp", "seq"), axis=0, tiled=True).astype(
-            jnp.float32
-        ),
-        lax.all_gather(shares[3].astype(jnp.bfloat16), ("dp", "seq"), axis=0, tiled=True).astype(
-            jnp.float32
-        ),
-        lax.all_gather(shares[4].astype(jnp.bfloat16), ("dp", "seq"), axis=0, tiled=True).astype(
-            jnp.float32
-        ),
-        lax.all_gather(shares[5].astype(jnp.bfloat16), ("dp", "seq"), axis=0, tiled=True).astype(
-            jnp.float32
-        ),
-        lax.all_gather(shares[6].astype(jnp.bfloat16), ("dp", "seq"), axis=0, tiled=True).astype(
-            jnp.float32
-        ),
-        lax.all_gather(shares[7].astype(jnp.bfloat16), ("dp", "seq"), axis=0, tiled=True).astype(
-            jnp.float32
-        ),
-    )
+    small = jnp.concatenate(
+        [grad_gain_one, grad_shift_one, grad_bias_in, grad_bias_out, grad_gain_two, grad_shift_two]
+    )
+    small = lax.psum(small, ("dp", "seq"))
+    sizes = {"dp": lax.axis_size("dp"), "seq": lax.axis_size("seq")}
+    wide = grad_weight_in.shape[1]
+    count = wide // 128
+    left = grad_weight_in.astype(jnp.bfloat16).reshape(features, count, 128).transpose(1, 0, 2)
+    right = grad_weight_out.astype(jnp.bfloat16).reshape(count, 128, features // 128, 128)
+    right = right.transpose(0, 2, 1, 3).reshape(count, features, 128)
+    packed = jnp.concatenate([left, right], axis=1)
+    group = max(1, sizes["dp"] * sizes["seq"] * 16 // packed.shape[1])
+    while packed.shape[1] * group % (sizes["dp"] * sizes["seq"] * 16):
+        group += 1
+    done = all_reduce(packed.reshape(count // group, -1, 128), sizes, [2, 4, 3, 2, 2, 2, 2, 3, 4, 2], 1)
+    done = done.reshape(packed.shape)
+    total_in = done[:, :features].transpose(1, 0, 2).reshape(features, wide).astype(jnp.float32)
+    total_out = done[:, features:].reshape(count, features // 128, 128, 128).transpose(0, 2, 1, 3)
+    total_out = total_out.reshape(wide, features).astype(jnp.float32)
+    cuts = [features, 2 * features, 2 * features + wide, 3 * features + wide, 4 * features + wide]
+    parts = jnp.split(small, cuts)
     return (
         layer_out,
         input_grad,
-        totals[0],
-        totals[1],
-        totals[2],
-        totals[3],
-        totals[4],
-        totals[5],
-        totals[6],
-        totals[7],
+        parts[0],
+        parts[1],
+        total_in,
+        parts[2],
+        total_out,
+        parts[3],
+        parts[4],
+        parts[5],
     )
 
 

time: 760 us -> 564 us (0.74)
  waiting for transfers between devices: 298 us -> 44.6 us
  blocking collectives: 163 us -> 58.9 us
  Pallas kernels: 0 us -> 90.3 us
  local copies, waits for them, and re-layouts: 60.4 us -> 138 us
  between operations: 15.3 us -> 1.91 us
  starting transfers between devices: 16.4 us -> 25.2 us
    reduce_scatter x2 -> x0, waiting for transfers between devices: 267 us -> none  [the longest x1 140 us: per_device(): lax.psum_scatter(grad_weight_out, ('dp', 'seq'), scatter_dimension=0, til...]
    unnamed x2 -> x0, blocking collectives: 107 us -> none
    pallas_call x0 -> x1, Pallas kernels: none -> 90.3 us  [all_reduce(): pl.pallas_call(functools.partial(ar_kernel, sizes, lags), name=name, out_...]
    psum x0 -> x1, blocking collectives: none -> 58.9 us  [per_device(): small = lax.psum(small, ('dp', 'seq'))]
    all_to_all x2 -> x0, blocking collectives: 56.5 us -> none  [the longest x1 29.3 us: spectral(): lax.all_to_all(columns, 'seq', split_axis=0, concat_axis=2, tiled=True)]
    unnamed x50 -> x39, local copies, waits for them, and re-layouts: 6.75 us -> 39.7 us
    convert_element_type x0 -> x4, local copies, waits for them, and re-layouts: none -> 30.3 us  [the longest x1 9.63 us: per_device(): done[:, :features].transpose(1, 0, 2).reshape(features, wide)]
    all_to_all x0 -> x2, waiting for transfers between devices: none -> 25.6 us  [the longest x1 25.6 us: spectral(): lax.all_to_all(columns, 'seq', split_axis=0, concat_axis=2, tiled=True)]
  transfers between devices with their start and end apart: 8 -> 6, of which waited for: 5 -> 3; matrix products, arithmetic and copies ran while one was open for 17% -> 30% of each run, Pallas kernels for 0% -> 16%
where the time goes in v1:
time: 564 us; the launch traced here: 554 us
  matrix products  161 us (29%)
  local copies, waits for them, and re-layouts  138 us (24%)
  Pallas kernels  90.3 us (16%)
  blocking collectives  58.9 us (10%)
  waiting for transfers between devices  44.6 us (8%)
  other arithmetic  34.3 us (6%)
  starting transfers between devices  25.2 us (4%)
    pallas_call x1, Pallas kernels, all_reduce(): pl.pallas_call(functools.partial(ar_kernel, sizes, lags), name=name, out_...  90.3 us
    psum x1, blocking collectives, per_device(): small = lax.psum(small, ('dp', 'seq'))  58.9 us
    unnamed x39, local copies, waits for them, and re-layouts  39.7 us
    dot_general x1, matrix products, dense_forward(): jnp.dot(normed, weight_in, preferred_element_type=jnp.float32) + bias_in  37.4 us
    dot_general x2, matrix products, contract_cols(): lax.dot_general(left, right, (((1,), (1,)), ((), ())), preferred_element_...  28 us
    all_to_all x1, waiting for transfers between devices, spectral(): lax.all_to_all(columns, 'seq', split_axis=0, concat_axis=2, tiled=True)  25.6 us
    dot_general x2, matrix products, contract_rows(): lax.dot_general(left, right, (((0,), (0,)), ((), ())), preferred_element_...  16.9 us
    dot_general x1, matrix products, per_device(): jnp.dot(grad_sin_rows.reshape(-1, features), hidden_sin, preferred_elemen...  13.9 us
  transfers between devices with their start and end apart: 6, of which 3 were waited for; matrix products, arithmetic and copies ran while one was open for 30% of the time, Pallas kernels for 16%

profile of v1, /device:TPU:0, one launch (start us, length us, event | category | flops | bytes accessed | tf_op | source)
XLA Modules:
  0.0 553.8 jit_solution(934462051311044596)
XLA Ops:
  2.2 11.5 %fusion.29 = bf16[128,8,768]{2,1,0:T(8,128)(2,1)S(1)} fusion(f32[128,8,768]{2,1,0:T(8,128)} %param.12, f32[128,8]{1,0:T(8,128)S(1)} %copy.156), kind=kOutput, calls=%fused_computation.81 | convolution fusion | flops 1216217088 | bytes 4722688 | tf_op jit(solution)/shard_map/dot_general | solution.py:161
  20.4 11.5 %fusion.30 = bf16[128,8,768]{2,1,0:T(8,128)(2,1)S(1)} fusion(f32[128,8,768]{2,1,0:T(8,128)} %param.12, f32[128,8]{1,0:T(8,128)S(1)} %copy.156), kind=kOutput, calls=%fused_computation.82 | convolution fusion | flops 1216217088 | bytes 4722688 | tf_op jit(solution)/shard_map/dot_general | solution.py:166
  34.3 6.2 %all-to-all-done = bf16[128,8,768]{0,1,2:T(8,128)(2,1)S(1)} async-done(((bf16[128,8,768]{0,1,2:T(8,128)(2,1)}), bf16[128,8,768]{0,1,2:T(8,128)(2,1)S(1)}, u32[]{:S(2)}, u32[]{:S(2)}) %all-to-all-start) | async-done | bytes 1572896 | tf_op jit(solution)/shard_map/all_to_all | solution.py:193
  45.8 6.1 %fusion.24 = f32[512,1536]{1,0:T(8,128)} fusion(bf16[192,8,4,128]{3,2,1,0:T(4,128)(2,1)S(1)} %bitcast.141), kind=kOutput, calls=%fused_computation.73 | convolution fusion | flops 809238528 | bytes 4718592 | tf_op jit(solution)/shard_map/dot_general | solution.py:174
  51.9 12.8 %all-to-all-done.1 = bf16[128,8,768]{0,1,2:T(8,128)(2,1)S(1)} async-done(((bf16[128,8,768]{0,1,2:T(8,128)(2,1)}), bf16[128,8,768]{0,1,2:T(8,128)(2,1)S(1)}, u32[]{:S(2)}, u32[]{:S(2)}) %all-to-all-start.1) | async-done | bytes 1572896 | tf_op jit(solution)/shard_map/all_to_all | solution.py:194
  66.5 4.9 fusion.11
  79.0 25.6 %all-to-all-done.2 = bf16[512,8,192]{2,1,0:T(8,128)(2,1)S(1)} async-done(((bf16[512,8,192]{2,1,0:T(8,128)(2,1)}), bf16[512,8,192]{2,1,0:T(8,128)(2,1)S(1)}, u32[]{:S(2)}, u32[]{:S(2)}) %all-to-all-start.2) | async-done | bytes 1572896 | tf_op jit(solution)/shard_map/all_to_all | solution.py:197
  120.1 37.4 %multiply_convert_fusion = (bf16[1024,3072]{1,0:T(8,128)(2,1)S(1)}, f32[1024,3072]{1,0:T(8,128)}, f32[1024,3072]{1,0:T(8,128)}) fusion(f32[3072]{0:T(1024)S(1)} %copy-done.9, bf16[768,3072]{1,0:T(8,128)(2,1)} %param.17, f32[128,8,768]{2,1,0:T(8,128)S(1)} %get-tuple-element.85, f32[768]{0:T(1024)S(1)} %copy-done.11, f32[768]{0:T(1024)S(1)} %copy-done.7, ...), kind=kOutput, calls=%fused_computation.4 | convolution fusion | flops 5043388416 | bytes 39348224 | tf_op jit(solution)/shard_map/dot_general | solution.py:207
  157.5 5.3 fusion.81
  169.3 7.0 %convolution_convert_fusion = bf16[3072,768]{1,0:T(8,128)(2,1)} fusion(bf16[1024,3072]{1,0:T(8,128)(2,1)S(1)} %get-tuple-element.82, f32[128,8,768]{2,1,0:T(8,128)S(1)} %get-tuple-element.79), kind=kOutput, calls=%fused_computation.21 | convolution fusion | flops 4834983936 | bytes 14155776 | tf_op jit(solution)/shard_map/dot_general | solution.py:145
  176.3 19.0 %convert_reduce_fusion = (f32[3072]{0:T(1024)S(1)}, bf16[1024,3072]{1,0:T(8,128)(2,1)}) fusion(f32[1024,3072]{1,0:T(8,128)} %get-tuple-element.83, bf16[3072,768]{1,0:T(8,128)(2,1)} %param.19, f32[128,8,768]{2,1,0:T(8,128)} %copy-done.2, f32[1024,3072]{1,0:T(8,128)} %get-tuple-element.94, f32[3072]{0:T(1024)S(1)} %copy-done.9), kind=kOutput, calls=%fused_computation.2 | convolution fusion | flops 4886098944 | bytes 39346176 | tf_op jit(solution)/shard_map/dot_general | solution.py:151
  195.3 9.0 %fusion.9 = (f32[768]{0:T(1024)S(1)}, f32[128,8]{1,0:T(8,128)S(1)}, f32[1024,768]{1,0:T(8,128)S(1)}) fusion(f32[128,8,768]{2,1,0:T(8,128)S(1)} %get-tuple-element.85, f32[128,8]{1,0:T(8,128)S(1)} %add_rsqrt_fusion.1, f32[128,8]{1,0:T(8,128)S(1)} %broadcast_multiply_fusion.4, f32[768]{0:T(1024)S(1)} %copy-done.7, bf16[1024,3072]{1,0:T(8,128)(2,1)} %get-tuple-element.99, ...), kind=kOutput, calls=%fused_computation.33 | convolution fusion | flops 4837341184 | bytes 17319936 | tf_op jit(solution)/shard_map/dot_general | solution.py:151
  206.5 4.8 fusion.76
  219.1 9.9 %convolution_convert_fusion.1 = bf16[768,3072]{1,0:T(8,128)(2,1)} fusion(bf16[1024,3072]{1,0:T(8,128)(2,1)} %get-tuple-element.99, f32[128,8,768]{2,1,0:T(8,128)S(1)} %get-tuple-element.85, f32[768]{0:T(1024)S(1)} %copy-done.11, f32[768]{0:T(1024)S(1)} %copy-done.7, f32[128,8]{1,0:T(8,128)S(1)} %add_rsqrt_fusion.1, f32[128,8]{1,0:T(8,128)S(1)} %broadcast_multiply_fusion.4), kind=kOutput, calls=%fused_computation.22 | convolution fusion | flops 4838129664 | bytes 14170112 | tf_op jit(solution)/shard_map/dot_general | solution.py:145
  229.0 6.6 %copy.177 = bf16[768,3072]{0,1:T(8,128)(2,1)} copy(bf16[768,3072]{1,0:T(8,128)(2,1)} %convolution_convert_fusion.1) | data formatting | bytes 9437184 | tf_op jit(solution)/shard_map/convert_element_type | solution.py:299
  235.6 6.7 %copy.178 = bf16[768,24,128]{2,0,1:T(8,128)(2,1)} copy(bf16[768,24,128]{0,2,1:T(8,128)(2,1)} %bitcast.123) | data formatting | bytes 9437184 | tf_op jit(solution)/shard_map/reshape | solution.py:299
  242.3 6.6 %copy.179 = bf16[3072,768]{0,1:T(8,128)(2,1)} copy(bf16[3072,768]{1,0:T(8,128)(2,1)} %convolution_convert_fusion) | data formatting | bytes 9437184 | tf_op jit(solution)/shard_map/convert_element_type | solution.py:300
  248.9 5.9 %copy.191 = bf16[96,8,24,128]{3,2,1,0:T(8,128)(2,1)} copy(bf16[96,8,24,128]{3,1,2,0:T(8,128)(2,1)} %bitcast.124) | data formatting | bytes 9437184
  254.8 7.0 %copy.180 = bf16[24,6,128,128]{3,2,1,0:T(8,128)(2,1)} copy(bf16[24,6,128,128]{2,0,3,1:T(8,128)(2,1)} %bitcast.125) | data formatting | bytes 9437184 | tf_op jit(solution)/shard_map/transpose | solution.py:301
  261.8 8.9 %pad_maximum_fusion.x_ref = bf16[24,1536,128]{2,1,0:T(8,128)(2,1)} fusion(bf16[24,768,128]{2,1,0:T(8,128)(2,1)} %bitcast.127, bf16[24,768,128]{2,1,0:T(8,128)(2,1)} %bitcast.126), kind=kLoop, calls=%fused_computation.19 | loop fusion | flops 18874368 | bytes 18874368 | tf_op jit(solution)/shard_map/concatenate | solution.py:302
  270.7 90.3 %ar.1 = bf16[24,1536,128]{2,1,0:T(8,128)(2,1)} custom-call(bf16[24,1536,128]{2,1,0:T(8,128)(2,1)} %pad_maximum_fusion.x_ref), custom_call_target="tpu_custom_call" | custom-call | tf_op jit(solution)/shard_map/ar/pallas_call | solution.py:113
  364.8 4.9 fusion.12
  377.3 10.4 %fusion.79 = (bf16[24,768,128]{2,1,0:T(8,128)(2,1)}, f32[768,24,128]{2,0,1:T(8,128)}) fusion(bf16[24,1536,128]{2,1,0:T(8,128)(2,1)} %ar.1), kind=kLoop, calls=%fused_computation.145 | loop fusion | flops 2359296 | bytes 23592960 | tf_op jit(solution)/shard_map/slice | solution.py:309
  387.7 7.4 %copy.182 = f32[24,6,128,128]{2,0,3,1:T(8,128)} copy(bf16[24,6,128,128]{3,2,1,0:T(8,128)(2,1)} %bitcast.122) | data formatting | bytes 14155776 | tf_op jit(solution)/shard_map/convert_element_type | solution.py:310
  395.2 9.5 %copy.212 = f32[96,8,24,128]{3,1,2,0:T(8,128)} copy(f32[96,8,24,128]{3,2,1,0:T(8,128)} %bitcast.119) | data formatting | bytes 18874368
  404.6 9.6 %copy.184 = f32[3072,768]{1,0:T(8,128)} copy(f32[3072,768]{0,1:T(8,128)} %bitcast.120) | data formatting | bytes 18874368
  414.2 9.6 %copy.181 = f32[768,24,128]{0,2,1:T(8,128)} copy(f32[768,24,128]{2,0,1:T(8,128)} %get-tuple-element.87) | data formatting | bytes 18874368 | tf_op jit(solution)/shard_map/convert_element_type | solution.py:308
  423.9 9.6 %copy.183 = f32[768,3072]{1,0:T(8,128)} copy(f32[768,3072]{0,1:T(8,128)} %bitcast.121) | data formatting | bytes 18874368
  433.5 7.2 %fusion.10 = bf16[512,1536]{1,0:T(8,128)(2,1)} fusion(bf16[192,8,4,128]{3,2,1,0:T(4,128)(2,1)} %bitcast.139), kind=kOutput, calls=%fused_computation.46 | convolution fusion | flops 811597824 | bytes 3145728 | tf_op jit(solution)/shard_map/dot_general | solution.py:275
  452.3 58.9 %psum.7 = f32[6912]{0:T(1024)S(1)} all-reduce(f32[6912]{0:T(1024)S(1)} %constant_dynamic-update-slice_fusion), channel_id=1, replica_groups=mesh['dp'=8,'seq'=4] {'dp','seq'}, use_global_device_ids=true, to_apply=%region_14.15 | all-reduce | flops 6912 | bytes 55296 | tf_op jit(solution)/shard_map/psum | solution.py:295
  519.5 12.9 %fusion.33 = f32[1024,768]{1,0:T(8,128)} fusion(bf16[1024,768]{1,0:T(8,128)(2,1)} %reshape.215), kind=kOutput, calls=%fused_computation.85 | convolution fusion | flops 1213857792 | bytes 4718592 | tf_op jit(solution)/shard_map/dot_general | solution.py:285
  539.8 13.9 %fusion.8 = f32[128,8,768]{2,1,0:T(8,128)} fusion(f32[128,8,768]{2,1,0:T(8,128)} %get-tuple-element.81, f32[1024,768]{1,0:T(8,128)} %fusion.33, bf16[1024,768]{1,0:T(8,128)(2,1)} %reshape.217, f32[128,8]{1,0:T(8,128)S(1)} %copy.156), kind=kOutput, calls=%fused_computation.30 | convolution fusion | flops 1216217088 | bytes 11014144 | tf_op jit(solution)/shard_map/dot_general | solution.py:288
  (87 shorter events, 94.9 us)
Async XLA Ops:
  15.9 24.6 %all-to-all-start = ((bf16[128,8,768]{0,1,2:T(8,128)(2,1)}), bf16[128,8,768]{0,1,2:T(8,128)(2,1)S(1)}, u32[]{:S(2)}, u32[]{:S(2)}) async-start(bf16[128,8,768]{0,1,2:T(8,128)(2,1)} %copy.157), calls=%async_computation | async-start | bytes 3145728 | tf_op jit(solution)/shard_map/all_to_all | solution.py:193
  40.5 24.1 %all-to-all-start.1 = ((bf16[128,8,768]{0,1,2:T(8,128)(2,1)}), bf16[128,8,768]{0,1,2:T(8,128)(2,1)S(1)}, u32[]{:S(2)}, u32[]{:S(2)}) async-start(bf16[128,8,768]{0,1,2:T(8,128)(2,1)} %copy.160), calls=%async_computation.1 | async-start | bytes 3145728 | tf_op jit(solution)/shard_map/all_to_all | solution.py:194
  64.6 1.9 copy-start.12
  75.2 29.4 %all-to-all-start.2 = ((bf16[512,8,192]{2,1,0:T(8,128)(2,1)}), bf16[512,8,192]{2,1,0:T(8,128)(2,1)S(1)}, u32[]{:S(2)}, u32[]{:S(2)}) async-start(bf16[512,8,192]{2,1,0:T(8,128)(2,1)} %copy.164), calls=%async_computation.2 | async-start | bytes 4194304 | tf_op jit(solution)/shard_map/all_to_all | solution.py:197
  115.9 41.6 %slice-start = ((s8[4718592]{0:T(1024)(128)(4,1)}), s8[4194304]{0:T(1024)(128)(4,1)S(1)}, s32[]{:S(2)}) async-start(s8[4718592]{0:T(1024)(128)(4,1)} %bitcast.142), calls=%async_computation.6 | async-start | bytes 8388608
  119.4 0.7 copy-start.7
  119.4 0.7 copy-start.9
  119.4 0.7 copy-start.11
  120.1 37.4 %slice-start.1 = ((s8[4718592]{0:T(1024)(128)(4,1)}), s8[524288]{0:T(1024)(128)(4,1)S(1)}, s32[]{:S(2)}) async-start(s8[4718592]{0:T(1024)(128)(4,1)} %bitcast.142), calls=%async_computation.7 | async-start | bytes 1048576
  120.1 37.4 %copy-start.10 = (f32[768]{0:T(1024)S(1)}, f32[768]{0:T(1024)}, u32[]{:S(2)}) copy-start(f32[768]{0:T(1024)} %param.20) | copy-start | bytes 9220
  162.8 1.9 copy-start
  162.8 1.9 copy-start.6
  164.7 1.9 copy-start.8
  169.3 7.0 %copy-start.2 = (f32[128,8,768]{2,1,0:T(8,128)}, f32[128,8,768]{2,1,0:T(8,128)S(1)}, u32[]{:S(2)}) copy-start(f32[128,8,768]{2,1,0:T(8,128)S(1)} %get-tuple-element.79) | copy-start | bytes 9437188
  204.3 1.7 copy-start.1
  214.6 146.4 %all-to-all-start.3 = ((bf16[128,8,768]{0,1,2:T(8,128)(2,1)}), bf16[128,8,768]{0,1,2:T(8,128)(2,1)}, u32[]{:S(2)}, u32[]{:S(2)}) async-start(bf16[128,8,768]{0,1,2:T(8,128)(2,1)} %copy.168), calls=%async_computation.3 | async-start | bytes 3145728 | tf_op jit(solution)/shard_map/all_to_all | solution.py:269
  363.7 1.2 copy-start.4
  373.5 74.3 %all-to-all-start.4 = ((bf16[512,8,192]{2,1,0:T(8,128)(2,1)}), bf16[512,8,192]{2,1,0:T(8,128)(2,1)S(1)}, u32[]{:S(2)}, u32[]{:S(2)}) async-start(bf16[512,8,192]{2,1,0:T(8,128)(2,1)} %copy.172), calls=%async_computation.4 | async-start | bytes 4194304 | tf_op jit(solution)/shard_map/all_to_all | solution.py:278
  423.9 9.6 %copy-start.5 = (f32[6912]{0:T(1024)S(1)}, f32[6912]{0:T(1024)}, u32[]{:S(2)}) copy-start(f32[6912]{0:T(1024)} %custom-call) | copy-start | bytes 82948
  447.7 64.6 %copy-start.3 = (bf16[512,8,192]{2,1,0:T(8,128)(2,1)}, bf16[512,8,192]{2,1,0:T(8,128)(2,1)S(1)}, u32[]{:S(2)}) copy-start(bf16[512,8,192]{2,1,0:T(8,128)(2,1)S(1)} %all-to-all-done.4) | copy-start | bytes 4718596
  447.7 84.8 %all-to-all-start.5 = ((bf16[512,8,192]{2,1,0:T(8,128)(2,1)}), bf16[512,8,192]{2,1,0:T(8,128)(2,1)}, u32[]{:S(2)}, u32[]{:S(2)}) async-start(bf16[512,8,192]{2,1,0:T(8,128)(2,1)} %copy.175), calls=%async_computation.5 | async-start | bytes 4194304 | tf_op jit(solution)/shard_map/all_to_all | solution.py:281

commit v2 on v0

v2 whole, which is shorter than its diff:
```python
import functools
import math

import jax
import jax.numpy as jnp
import numpy as np
from jax import lax
from jax.experimental import pallas as pl
from jax.experimental.pallas import tpu as pltpu
from jax.sharding import PartitionSpec as P

EPSILON = 1e-05
MESH = pl.DeviceIdType.MESH
LANES = 128
WIDE = 256
BF16 = jnp.bfloat16
F32 = jnp.float32


def dft_tables(count):
    index = np.arange(count, dtype=np.int64)
    turns = (index[:, None] * index[None, :] % count).astype(np.float32)
    angle = (turns * np.float32(2.0 * math.pi / count)).astype(np.float64)
    return np.cos(angle).astype(np.float32), np.sin(angle).astype(np.float32)


def aligned(value, step):
    return pl.multiple_of(value, step)


def bit_of(value, k):
    return (value // k) % 2


def flipped(value, k):
    return value + k * (1 - 2 * bit_of(value, k))


def axis_bits(axis, size):
    return [(axis, 1 << b) for b in range(size.bit_length() - 1)]


class Cube:
    def __init__(self, sizes):
        dp, seq = sizes
        bits = axis_bits(1, seq) + axis_bits(0, dp)
        first, rest = bits[:1], bits[1:]
        self.orders = [
            first + rest,
            first + [rest[1], rest[0]] + rest[2:],
            first + [rest[2], rest[0], rest[1]] + rest[3:],
        ]
        self.bits = bits
        self.stages = len(bits)
        self.me = (lax.axis_index("dp"), lax.axis_index("seq"))

    def value(self, bit):
        return bit_of(self.me[bit[0]], bit[1])

    def partner(self, bit):
        axis, k = bit
        other = flipped(self.me[axis], k)
        return (other, self.me[1]) if axis == 0 else (self.me[0], other)

    def offset(self, order, level, rows):
        total = 0
        for s in range(level):
            total = total + self.value(self.orders[order][s]) * (rows >> (s + 1))
        return total


class Exchange:
    def __init__(self, size, rows, buf, send, recv):
        self.size, self.rows, self.buf, self.send_sem, self.recv_sem = size, rows, buf, send, recv
        self.dp, self.q = lax.axis_index("dp"), lax.axis_index("seq")
        self.order = [1 << b for b in reversed(range(size.bit_length() - 1))]

    def owner(self, pattern):
        index = self.q
        for k in self.order:
            if pattern & k:
                index = flipped(index, k)
        return index

    def copy(self, slot, pattern):
        hop = pattern & -pattern
        place = pl.ds(aligned(self.owner(pattern - hop) * self.rows, self.rows), self.rows)
        ref = self.buf.at[slot, place]
        return pltpu.make_async_remote_copy(
            src_ref=ref,
            dst_ref=ref,
            send_sem=self.send_sem.at[slot, pattern],
            recv_sem=self.recv_sem.at[slot, pattern],
            device_id=(self.dp, flipped(self.q, hop)),
            device_id_type=MESH,
        )

    def patterns(self, far):
        return range(1, self.size) if far else range(1, 2)

    def start_own(self, slot, far):
        for pattern in self.patterns(far):
            if pattern & (pattern - 1) == 0:
                self.copy(slot, pattern).start()

    def forward(self, slot):
        for pattern in self.patterns(True):
            if pattern & 1 == 0:
                self.copy(slot, pattern).wait_recv()
                for k in self.order:
                    if k < (pattern & -pattern):
                        self.copy(slot, pattern | k).start()

    def wait_near(self, slot, far):
        for pattern in self.patterns(far):
            if pattern & 1:
                self.copy(slot, pattern).wait_recv()

    def wait_sends(self, slot, far):
        for pattern in self.patterns(far):
            self.copy(slot, pattern).wait_send()


def greet(partners):
    barrier = pltpu.get_barrier_semaphore()
    for partner in partners:
        pl.semaphore_signal(barrier, inc=1, device_id=partner, device_id_type=MESH)
    pl.semaphore_wait(barrier, len(partners))


def rank_slots(count_ref, length_ref, perm_s, slen_s, slots):
    count = count_ref[0]
    live = [jnp.where(i < count, length_ref[i], 0) for i in range(slots)]
    ranks = []
    for i in range(slots):
        rank = 0
        for k in range(slots):
            if k != i:
                ahead = live[k] >= live[i] if k < i else live[k] > live[i]
                rank = rank + jnp.where(ahead, 1, 0)
        ranks.append(rank)
    for j in range(slots):
        perm, length = 0, 0
        for i in range(slots):
            here = ranks[i] == j
            perm = perm + jnp.where(here, i, 0)
            length = length + jnp.where(here, live[i], 0)
        perm_s[j] = perm
        slen_s[j] = length


def live_rows(slen_s, slot, first, rows):
    position = first + lax.broadcasted_iota(jnp.int32, (rows, 1), 0)
    return position < slen_s[slot]


def fold8(values):
    rows, lanes = values.shape
    return values.reshape(rows // 8, 8, lanes).sum(axis=0)


def normalize(values):
    center = values - jnp.mean(values, axis=-1, keepdims=True)
    spread = jnp.mean(center * center, axis=-1, keepdims=True)
    inverse = lax.rsqrt(spread + EPSILON)
    return center * inverse, inverse


def norm_back(grad_hat, normal, inverse):
    first = jnp.mean(grad_hat, axis=-1, keepdims=True)
    second = jnp.mean(grad_hat * normal, axis=-1, keepdims=True)
    return inverse * (grad_hat - first - normal * second)


def mix_slot(slot, far, exchange, tables, buf, uv, place):
    rows = exchange.rows
    if far:
        table, block = tables[...], buf[slot]
    else:
        base = aligned(exchange.q // 2 * (2 * rows), 2 * rows)
        table, block = tables[:, pl.ds(base, 2 * rows)], buf[slot, pl.ds(base, 2 * rows), :]
    both = jnp.dot(table, block, preferred_element_type=F32).astype(BF16)
    width = both.shape[1]
    uv[pl.ds(place, rows), :width] = both[:rows]
    uv[pl.ds(place, rows), width:] = both[rows:]


def forward_kernel(cfg, *refs):
    sizes, far_slots, slots, group = cfg
    (
        count_ref, length_ref, gain_one, shift_one, bias_in, bias_out, gain_two, shift_two,
        x_hbm, cot_hbm, wi_hbm, wo_hbm, sc_hbm, hc_hbm,
        act_o, dg_o, nrm_o, sum_o, gs_o, lo_o, part_o,
        perm_s, slen_s, x_v, cot_v, wi_v, wo_v, sc_v, hc_v, buf, uv, sum_v, nrm_v, act_v, dg_v, gs_v, lo_v,
        load_sem, out_sem, send_sem, recv_sem,
    ) = refs
    rows, _, features = x_v.shape
    wide = wi_v.shape[1]
    seq_total = rows * sizes[1]
    scale = 1.0 / math.sqrt(features * seq_total)
    exchange = Exchange(sizes[1], rows, buf, send_sem, recv_sem)
    q = exchange.q
    first = q * rows
    loads = [
        pltpu.make_async_copy(x_hbm, x_v, load_sem.at[0]),
        pltpu.make_async_copy(sc_hbm.at[q], sc_v, load_sem.at[1]),
        pltpu.make_async_copy(hc_hbm, hc_v, load_sem.at[2]),
        pltpu.make_async_copy(wi_hbm, wi_v, load_sem.at[3]),
        pltpu.make_async_copy(wo_hbm, wo_v, load_sem.at[4]),
        pltpu.make_async_copy(cot_hbm, cot_v, load_sem.at[5]),
    ]
    for load in loads:
        load.start()
    rank_slots(count_ref, length_ref, perm_s, slen_s, slots)
    greet([(exchange.dp, flipped(q, k)) for k in exchange.order])
    loads[0].wait()

    def prepare(slot):
        value = jnp.where(live_rows(slen_s, slot, first, rows), x_v[:, perm_s[slot], :], 0.0)
        sum_v[pl.ds(aligned(slot * rows, rows), rows), :] = value
        buf[slot, pl.ds(aligned(first, rows), rows), :] = value.astype(BF16)

    def prepare_far(i, _):
        slot = far_slots - 1 - i
        prepare(slot)
        exchange.start_own(slot, True)
        return 0

    def prepare_near(i, _):
        prepare(far_slots + i)
        exchange.start_own(far_slots + i, False)
        return 0

    lax.fori_loop(0, far_slots, prepare_far, 0)
    lax.fori_loop(0, slots - far_slots, prepare_near, 0)
    part_o[...] = jnp.zeros_like(part_o)
    for load in loads[1:3]:
        load.wait()

    batch = group * rows
    span = min(3 * WIDE, wide)

    def outs(base):
        place = pl.ds(base, batch)
        copies = [
            pltpu.make_async_copy(nrm_v.at[place], nrm_o.at[place], out_sem.at[0]),
            pltpu.make_async_copy(sum_v.at[place], sum_o.at[place], out_sem.at[1]),
            pltpu.make_async_copy(gs_v.at[place], gs_o.at[place], out_sem.at[2]),
            pltpu.make_async_copy(lo_v.at[place], lo_o.at[place], out_sem.at[3]),
        ]
        for n in range(wide // WIDE):
            cut = pl.ds(n * WIDE, WIDE)
            copies.append(pltpu.make_async_copy(act_v.at[place, cut], act_o.at[n, place], out_sem.at[4]))
            copies.append(pltpu.make_async_copy(dg_v.at[place, cut], dg_o.at[n, place], out_sem.at[5]))
        return copies

    def mixing(slot0, flags):
        for i, far in enumerate(flags):
            exchange.wait_near(slot0 + i, far)
            mix_slot(slot0 + i, far, exchange, sc_v, buf, uv, i * rows)

    def dense(slot0):
        base = aligned(slot0 * rows, batch)
        place = pl.ds(base, batch)
        uv_out = jnp.dot(uv[...], hc_v[...], preferred_element_type=F32)
        sum_v[place, :] = sum_v[place, :] + (uv_out * scale).astype(BF16).astype(F32)

        def norm_one(i, _):
            here = pl.ds(aligned(base + i * rows, rows), rows)
            hat, _ = normalize(sum_v[here, :])
            nrm_v[here, :] = (hat * gain_one[...] + shift_one[...]).astype(BF16)
            return 0

        lax.fori_loop(0, group, norm_one, 0)

        def expand(n, _):
            cut = pl.ds(aligned(n * span, span), span)
            hidden = jnp.dot(nrm_v[place, :], wi_v[:, cut], preferred_element_type=F32) + bias_in[:, cut]
            gate = 0.5 + 0.5 * lax.erf(hidden * math.sqrt(0.5))
            slope = gate + hidden * (jnp.exp(hidden * hidden * -0.5) * (1.0 / math.sqrt(2.0 * math.pi)))
            act_v[place, cut] = (hidden * gate).astype(BF16)
            dg_v[place, cut] = slope.astype(BF16)
            return 0

        lax.fori_loop(0, wide // span, expand, 0)
        lo_v[place, :] = jnp.dot(act_v[place, :], wo_v[...], preferred_element_type=F32)

        def norm_two(i, _):
            here = pl.ds(aligned(base + i * rows, rows), rows)
            slot = slot0 + i
            live = live_rows(slen_s, slot, first, rows)
            hat, inverse = normalize(sum_v[here, :] + (lo_v[here, :] + bias_out[...]))
            grad = jnp.where(live, cot_v[:, perm_s[slot], :], 0.0)
            lo_v[here, :] = jnp.where(live, hat * gain_two[...] + shift_two[...], 0.0)
            part_o[0:8, :] = part_o[0:8, :] + fold8(grad * hat)
            part_o[8:16, :] = part_o[8:16, :] + fold8(grad)
            second = norm_back(grad * gain_two[...], hat, inverse)
            gs_v[here, :] = second
            part_o[16:24, :] = part_o[16:24, :] + fold8(second.astype(BF16).astype(F32))
            return 0

        lax.fori_loop(0, group, norm_two, 0)
        for copy in outs(base):
            copy.start()

    count = slots // group
    near_groups = (slots - far_slots) // group
    work = list(range(count - near_groups, count)) + list(range(count - near_groups - 1, -1, -1))
    ready = set()

    def bring(g):
        for slot in range(g * group + group - 1, g * group - 1, -1):
            if slot < far_slots and slot not in ready:
                ready.add(slot)
                exchange.forward(slot)

    for at, g in enumerate(work):
        bring(g)
        mixing(g * group, [g * group + i < far_slots for i in range(group)])
        if at == 0:
            for load in loads[3:]:
                load.wait()
        if at + 1 < len(work):
            bring(work[at + 1])
        dense(g * group)

    for slot in range(slots):
        exchange.wait_sends(slot, slot < far_slots)
    for g in range(count):
        for copy in outs(g * batch):
            copy.wait()


def backward_kernel(cfg, *refs):
    sizes, far_slots, slots, group, lags, plan = cfg
    cube = Cube(sizes)
    S = cube.stages
    (
        count_ref, length_ref, gain_one, part_ref,
        act_hbm, dg_hbm, nrm_hbm, sum_hbm, gs_hbm, wi_hbm, wo_hbm, sc_hbm, hc_hbm,
        full_o, ig_o, small_o,
        perm_s, slen_s, gs_v, sum_v, nrm_v, gb_v, gh_v, gn_v, act_v, dg_v, wi_v, wo_v, sc_v, hc_v, buf, uv, ig_v,
        bin_v, one_v, small_v, part_v, full,
    ) = refs[: 16 + 22]
    landed = refs[38 : 38 + S]
    (
        small_recv, load_sem, sum_sem, stream_sem, out_sem, ig_sem, send_sem, recv_sem,
        rs_s, rs_r, ag_s, ag_r, sm_s, sm_r,
    ) = refs[38 + S :]
    ticks, tick_rows, _ = part_v.shape
    parts = 3
    message = tick_rows // parts
    chunks = act_hbm.shape[0]
    per_tick = chunks // ticks
    total = ticks * parts
    features = nrm_v.shape[1]
    rows = gs_v.shape[0] // slots
    scale = 1.0 / math.sqrt(features * rows * sizes[1])
    exchange = Exchange(sizes[1], rows, buf, send_sem, recv_sem)
    q = exchange.q
    first = q * rows
    loads = [
        pltpu.make_async_copy(gs_hbm, gs_v, load_sem.at[0]),
        pltpu.make_async_copy(nrm_hbm, nrm_v, load_sem.at[1]),
        pltpu.make_async_copy(sc_hbm.at[q], sc_v, load_sem.at[2]),
        pltpu.make_async_copy(hc_hbm, hc_v, load_sem.at[3]),
    ]

    def sum_copy(i):
        slot = jnp.where(i < far_slots, far_slots - 1 - i, i)
        place = pl.ds(aligned(slot * rows, rows), rows)
        return pltpu.make_async_copy(sum_hbm.at[place], sum_v.at[i % 2], sum_sem.at[i % 2])

    def streams(n, slot):
        cut = pl.ds(aligned(n * WIDE, WIDE), WIDE)
        return [
            pltpu.make_async_copy(wo_hbm.at[cut], wo_v.at[slot], stream_sem.at[0, slot]),
            pltpu.make_async_copy(dg_hbm.at[n], dg_v.at[slot], stream_sem.at[1, slot]),
            pltpu.make_async_copy(act_hbm.at[n], act_v.at[slot], stream_sem.at[2, slot]),
            pltpu.make_async_copy(wi_hbm.at[:, cut], wi_v.at[slot], stream_sem.at[3, slot]),
        ]

    loads[0].start()
    for copy in streams(0, 0):
        copy.start()
    for load in loads[1:]:
        load.start()
    for i in range(2):
        sum_copy(i).start()
    rank_slots(count_ref, length_ref, perm_s, slen_s, slots)
    greet([cube.partner(bit) for bit in cube.bits])

    def rs(m, t, j, s):
        bit = cube.orders[j][s]
        half = message >> (s + 1)
        off = j * message + cube.offset(j, s, message) + (1 - cube.value(bit)) * half
        return pltpu.make_async_remote_copy(
            src_ref=part_v.at[t, pl.ds(aligned(off, 16), half)],
            dst_ref=landed[s].at[m],
            send_sem=rs_s.at[s, m],
            recv_sem=rs_r.at[s, m],
            device_id=cube.partner(bit),
            device_id_type=MESH,
        )

    def ag(m, t, j, s):
        bit = cube.orders[j][s]
        half = message >> (s + 1)
        off = j * message + cube.offset(j, s + 1, message)
        ref = full.at[t, pl.ds(aligned(off, 16), half)]
        return pltpu.make_async_remote_copy(
            src_ref=ref,
            dst_ref=ref,
            send_sem=ag_s.at[s, m],
            recv_sem=ag_r.at[s, m],
            device_id=cube.partner(bit),
            device_id_type=MESH,
        )

    def add(m, t, j, s):
        half = message >> (s + 1)
        place = pl.ds(aligned(j * message + cube.offset(j, s + 1, message), 16), half)
        sent = part_v[t, place, :].astype(F32) + landed[s][m].astype(F32)
        target = full if s == S - 1 else part_v
        target[t, place, :] = sent.astype(BF16)

    def out(t, j):
        place = pl.ds(j * message, message)
        return pltpu.make_async_copy(full.at[t, place], full_o.at[t, place], out_sem.at[t, j])

    def event(k, m, t, j):
        if k == 0:
            rs(m, t, j, 0).start()
        elif k <= S:
            rs(m, t, j, k - 1).wait()
            add(m, t, j, k - 1)
            (rs(m, t, j, k) if k < S else ag(m, t, j, S - 1)).start()
        elif k < 2 * S:
            s = 2 * S - k
            ag(m, t, j, s).wait()
            ag(m, t, j, s - 1).start()
        else:
            ag(m, t, j, 0).wait()
            out(t, j).start()

    when = [2]
    for lag in lags:
        when.append(when[-1] + lag)

    def events(tick, j):
        for k in reversed(range(2 * S + 1)):
            t = tick + (j - when[k]) // parts
            jj = (j - when[k]) % parts
            pl.when((t >= 0) & (t < ticks))(functools.partial(event, k, t * parts + jj, t, jj))

    bin_v[...] = jnp.zeros_like(bin_v)
    one_v[...] = jnp.zeros_like(one_v)
    gn_v[...] = jnp.zeros_like(gn_v)
    small_v[...] = jnp.zeros_like(small_v)
    loads[0].wait()
    gb_v[...] = gs_v[...].astype(BF16)

    def contract(left, right, dims):
        return lax.dot_general(left, right, ((dims, dims), ((), ())), preferred_element_type=F32)

    def pull(n, slot):
        wo_copy, dg_copy, _, _ = streams(n, slot)
        wo_copy.wait()
        dg_copy.wait()
        pulled = contract(gb_v[...], wo_v[slot], (1,)) * dg_v[slot].astype(F32)
        pulled = pulled.astype(BF16)
        gh_v[...] = pulled
        bin_v[n] = fold8(pulled.astype(F32))

    def weigh_out(n, slot, t, base):
        streams(n, slot)[2].wait()
        grad = contract(act_v[slot], gb_v[...], (0,)).astype(BF16)
        for i in range(features // LANES):
            part_v[t, pl.ds(base + 2 * features + i * WIDE, WIDE), :] = grad[:, i * LANES : (i + 1) * LANES]

    def weigh_in(n, slot, t, base):
        streams(n, slot)[3].wait()
        grad = contract(nrm_v[...], gh_v[...], (0,)).astype(BF16)
        for i in range(WIDE // LANES):
            part_v[t, pl.ds(base + i * features, features), :] = grad[:, i * LANES : (i + 1) * LANES]

        def spread(i, _):
            here = pl.ds(aligned(i * (slots // 2) * rows, rows), slots // 2 * rows)
            gn_v[here, :] = gn_v[here, :] + contract(gh_v[here, :], wi_v[slot], (1,))
            return 0

        lax.fori_loop(0, 2, spread, 0)

    def back_slot(slot, i):
        here = pl.ds(aligned(slot * rows, rows), rows)
        sum_copy(i).wait()
        hat, inverse = normalize(sum_v[i % 2])
        grad = gn_v[here, :]
        one_v[0:8, :] = one_v[0:8, :] + fold8(grad * hat)
        one_v[8:16, :] = one_v[8:16, :] + fold8(grad)
        grad = gs_v[here, :] + norm_back(grad * gain_one[...], hat, inverse)
        gs_v[here, :] = grad
        buf[slot, pl.ds(aligned(first, rows), rows), :] = grad.astype(BF16)
        pl.when(i + 2 < slots)(lambda: sum_copy(i + 2).start())

    def back_far(i, _):
        slot = far_slots - 1 - i
        back_slot(slot, i)
        exchange.start_own(slot, True)
        return 0

    def back_near(i, _):
        back_slot(far_slots + i, far_slots + i)
        exchange.start_own(far_slots + i, False)
        return 0

    def back_all():
        lax.fori_loop(0, far_slots, back_far, 0)
        lax.fori_loop(0, slots - far_slots, back_near, 0)

    def small_copy(s):
        return pltpu.make_async_remote_copy(
            src_ref=small_v.at[s],
            dst_ref=small_recv.at[s],
            send_sem=sm_s.at[s],
            recv_sem=sm_r.at[s],
            device_id=cube.partner(cube.bits[s]),
            device_id_type=MESH,
        )

    def small_start():
        row = 0
        vectors = [one_v[0:8, :], one_v[8:16, :]] + [bin_v[n] for n in range(chunks)]
        vectors += [part_ref[16:24, :], part_ref[0:8, :], part_ref[8:16, :]]
        for vector in vectors:
            vector = jnp.sum(vector, axis=0, keepdims=True)
            for i in range(vector.shape[1] // LANES):
                small_v[0, row : row + 1, :] = vector[:, i * LANES : (i + 1) * LANES]
                row += 1
        small_copy(0).start()

    def small_step(s):
        small_copy(s).wait()
        if s + 1 < S:
            small_v[s + 1] = small_v[s] + small_recv[s]
            small_copy(s + 1).start()
        else:
            small_o[...] = small_v[s] + small_recv[s]

    def grad_copy(g, i):
        return pltpu.make_async_copy(
            ig_v.at[i % 2], ig_o.at[pl.ds(aligned(g * group * rows, group * rows), group * rows)], ig_sem.at[i % 2]
        )

    def mixing(g, i):
        if i == 0:
            for load in loads[2:]:
                load.wait()
        if i >= 2:
            grad_copy(work[i - 2], i).wait()
        for k in range(group):
            far = g * group + k < far_slots
            exchange.wait_near(g * group + k, far)
            mix_slot(g * group + k, far, exchange, sc_v, buf, uv, k * rows)
        ig_v[i % 2] = jnp.dot(uv[...], hc_v[...], preferred_element_type=F32)

        def finish(k, _):
            slot = g * group + k
            here = pl.ds(aligned(slot * rows, rows), rows)
            local = pl.ds(aligned(k * rows, rows), rows)
            grad = gs_v[here, :] + ig_v[i % 2, local, :] * scale
            ig_v[i % 2, local, :] = jnp.where(live_rows(slen_s, slot, first, rows), grad, 0.0)
            return 0

        lax.fori_loop(0, group, finish, 0)
        grad_copy(g, i).start()

    count = slots // group
    near_groups = (slots - far_slots) // group
    work = list(range(count - near_groups, count)) + list(range(count - near_groups - 1, -1, -1))

    def forward_slots(g):
        for slot in range(g * group + group - 1, g * group - 1, -1):
            if slot < far_slots:
                exchange.forward(slot)

    tasks = {}

    def task(at, fn):
        tasks.setdefault(at, []).append(fn)

    task(ticks, back_all)
    task(ticks, small_start)
    for s in range(S):
        task(ticks + 1 + s, functools.partial(small_step, s))
    for i, g in enumerate(work):
        task(ticks + plan[i][0], functools.partial(forward_slots, g))
        task(ticks + plan[i][1], functools.partial(mixing, g, i))
    last = ticks + -(-(when[-1] + 1) // parts)
    last = max(last, max(tasks) + 1)

    def body(tick, _):
        def compute():
            for u in range(per_tick):
                n = tick * per_tick + u
                slot = lax.rem(n, 2)
                for copy in streams(n + 1, 1 - slot):
                    pl.when(n + 1 < chunks)(copy.start)
                base = u * (tick_rows // per_tick)
                pull(n, slot)
                if u == 0:
                    events(tick, 0)
                    pl.when(tick == 0)(loads[1].wait)
                weigh_in(n, slot, tick, base)
                if u == 0:
                    events(tick, 1)
                weigh_out(n, slot, tick, base)
            events(tick, 2)

        def drain():
            for j in range(parts):
                events(tick, j)
            for at, fns in sorted(tasks.items()):
                @pl.when(tick == at)
                def _():
                    for fn in fns:
                        fn()

        pl.when(tick < ticks)(compute)
        pl.when(tick >= ticks)(drain)
        return 0

    lax.fori_loop(0, last, body, 0)
    for slot in range(slots):
        exchange.wait_sends(slot, slot < far_slots)
    for i in range(max(0, count - 2), count):
        grad_copy(work[i], i).wait()

    def finish_out(t, _):
        for j in range(parts):
            out(t, j).wait()
        return 0

    lax.fori_loop(0, ticks, finish_out, 0)


def widen_kernel(full_ref, wi_ref, wo_ref):
    features = wi_ref.shape[0]
    for i in range(WIDE // LANES):
        wi_ref[:, i * LANES : (i + 1) * LANES] = full_ref[0, pl.ds(i * features, features), :].astype(F32)
    for i in range(features // LANES):
        start = 2 * features + i * WIDE
        wo_ref[:, i * LANES : (i + 1) * LANES] = full_ref[0, pl.ds(start, WIDE), :].astype(F32)


def restore_kernel(slots, count_ref, length_ref, lo_ref, ig_ref, lo_out, ig_out, perm_s, slen_s):
    rank_slots(count_ref, length_ref, perm_s, slen_s, slots)
    for j in range(slots):
        lo_out[:, perm_s[j], :] = lo_ref[j]
        ig_out[:, perm_s[j], :] = ig_ref[j]


LAGS = [3, 9, 6, 4, 3, 3, 4, 6, 9, 3]
ANY = pl.BlockSpec(memory_space=pl.ANY)
SMEM = pl.BlockSpec(memory_space=pltpu.SMEM)
VMEM = pl.BlockSpec(memory_space=pltpu.VMEM)
DMA = pltpu.SemaphoreType.DMA
PLAN = [(1, 3), (1, 4), (6, 8), (8, 10)]


def per_device(
    inputs, item_counts, lengths, gain_one, shift_one, weight_in, bias_in, weight_out, bias_out, gain_two, shift_two, cotangent
):
    rows, slots, features = inputs.shape
    wide = weight_in.shape[1]
    sizes = (lax.axis_size("dp"), lax.axis_size("seq"))
    devices = sizes[0] * sizes[1]
    seq_total = rows * sizes[1]
    flat = rows * slots
    far_slots, group = slots, 2
    chunks = wide // WIDE
    chunk_rows = 2 * features * WIDE // LANES
    per_tick = 1
    while chunks % per_tick or chunk_rows * per_tick % (devices * 16 * 3):
        per_tick += 1
    ticks = chunks // per_tick
    tick_rows = chunk_rows * per_tick
    message = tick_rows // 3

    seq_cos, seq_sin = dft_tables(seq_total)
    hid_cos, hid_sin = dft_tables(features)
    seq_table = np.concatenate([seq_cos.reshape(sizes[1], rows, seq_total), seq_sin.reshape(sizes[1], rows, seq_total)], axis=1)
    seq_table = jnp.asarray(seq_table.astype(jnp.bfloat16))
    hid_table = jnp.asarray(np.concatenate([hid_cos, -hid_sin], axis=0).astype(jnp.bfloat16))
    vec = lambda v: v.reshape(1, -1)
    shape = jax.ShapeDtypeStruct
    batch = group * rows

    act, dg, nrm, summed, second, lo, part = pl.pallas_call(
        functools.partial(forward_kernel, (sizes, far_slots, slots, group)),
        name="forward",
        out_shape=(
            shape((chunks, flat, WIDE), BF16),
            shape((chunks, flat, WIDE), BF16),
            shape((flat, features), BF16),
            shape((flat, features), F32),
            shape((flat, features), F32),
            shape((flat, features), F32),
            shape((24, features), F32),
        ),
        in_specs=[SMEM] * 2 + [VMEM] * 6 + [ANY] * 6,
        out_specs=[ANY] * 6 + [VMEM],
        scratch_shapes=[
            pltpu.SMEM((slots,), jnp.int32),
            pltpu.SMEM((slots,), jnp.int32),
            pltpu.VMEM((rows, slots, features), F32),
            pltpu.VMEM((rows, slots, features), F32),
            pltpu.VMEM((features, wide), BF16),
            pltpu.VMEM((wide, features), BF16),
            pltpu.VMEM((2 * rows, seq_total), BF16),
            pltpu.VMEM((2 * features, features), BF16),
            pltpu.VMEM((slots, seq_total, features), BF16),
            pltpu.VMEM((batch, 2 * features), BF16),
            pltpu.VMEM((flat, features), F32),
            pltpu.VMEM((flat, features), BF16),
            pltpu.VMEM((flat, wide), BF16),
            pltpu.VMEM((flat, wide), BF16),
            pltpu.VMEM((flat, features), F32),
            pltpu.VMEM((flat, features), F32),
            DMA((6,)),
            DMA((6,)),
            DMA((slots, sizes[1])),
            DMA((slots, sizes[1])),
        ],
        compiler_params=pltpu.CompilerParams(collective_id=1, has_side_effects=True, vmem_limit_bytes=62 << 20),
    )(
        item_counts, lengths, vec(gain_one), vec(shift_one), vec(bias_in), vec(bias_out), vec(gain_two), vec(shift_two),
        inputs, cotangent, weight_in, weight_out, seq_table, hid_table,
    )

    stages = (devices).bit_length() - 1
    lags = (LAGS[:stages] + [2] * stages)[:stages] + ([2] * stages + LAGS[-stages:])[-stages:]
    full, grad, small = pl.pallas_call(
        functools.partial(backward_kernel, (sizes, far_slots, slots, group, lags, PLAN)),
        name="backward",
        out_shape=(
            shape((ticks, tick_rows, LANES), BF16),
            shape((flat, features), F32),
            shape((64, LANES), F32),
        ),
        in_specs=[SMEM] * 2 + [VMEM] * 2 + [ANY] * 9,
        out_specs=[ANY] * 2 + [VMEM],
        scratch_shapes=[
            pltpu.SMEM((slots,), jnp.int32),
            pltpu.SMEM((slots,), jnp.int32),
            pltpu.VMEM((flat, features), F32),
            pltpu.VMEM((2, rows, features), F32),
            pltpu.VMEM((flat, features), BF16),
            pltpu.VMEM((flat, features), BF16),
            pltpu.VMEM((flat, WIDE), BF16),
            pltpu.VMEM((flat, features), F32),
            pltpu.VMEM((2, flat, WIDE), BF16),
            pltpu.VMEM((2, flat, WIDE), BF16),
            pltpu.VMEM((2, features, WIDE), BF16),
            pltpu.VMEM((2, WIDE, features), BF16),
            pltpu.VMEM((2 * rows, seq_total), BF16),
            pltpu.VMEM((2 * features, features), BF16),
            pltpu.VMEM((slots, seq_total, features), BF16),
            pltpu.VMEM((batch, 2 * features), BF16),
            pltpu.VMEM((2, batch, features), F32),
            pltpu.VMEM((chunks, 8, WIDE), F32),
            pltpu.VMEM((16, features), F32),
            pltpu.VMEM((stages, 64, LANES), F32),
            pltpu.VMEM((ticks, tick_rows, LANES), BF16),
            pltpu.VMEM((ticks, tick_rows, LANES), BF16),
        ]
        + [pltpu.VMEM((ticks * 3, message >> (s + 1), LANES), BF16) for s in range(stages)]
        + [
            pltpu.VMEM((stages, 64, LANES), F32),
            DMA((4,)),
            DMA((2,)),
            DMA((4, 2)),
            DMA((ticks, 3)),
            DMA((2,)),
            DMA((slots, sizes[1])),
            DMA((slots, sizes[1])),
            DMA((stages, ticks * 3)),
            DMA((stages, ticks * 3)),
            DMA((stages, ticks * 3)),
            DMA((stages, ticks * 3)),
            DMA((stages,)),
            DMA((stages,)),
        ],
        compiler_params=pltpu.CompilerParams(collective_id=2, has_side_effects=True, vmem_limit_bytes=62 << 20),
    )(
        item_counts, lengths, vec(gain_one), part, act, dg, nrm, summed, second, weight_in, weight_out, seq_table, hid_table,
    )

    wi_grad, wo_grad = pl.pallas_call(
        widen_kernel,
        name="widen",
        grid=(chunks,),
        out_shape=(shape((features, wide), F32), shape((wide, features), F32)),
        in_specs=[pl.BlockSpec((1, chunk_rows, LANES), lambda n: (n, 0, 0))],
        out_specs=(
            pl.BlockSpec((features, WIDE), lambda n: (0, n)),
            pl.BlockSpec((WIDE, features), lambda n: (n, 0)),
        ),
    )(full.reshape(chunks, chunk_rows, LANES))

    step = 16
    lo, grad = lo.reshape(slots, rows, features), grad.reshape(slots, rows, features)
    layer_out, input_grad = pl.pallas_call(
        functools.partial(restore_kernel, slots),
        name="restore",
        grid=(rows // step,),
        out_shape=(shape(inputs.shape, F32), shape(inputs.shape, F32)),
        in_specs=[SMEM] * 2 + [pl.BlockSpec((slots, step, features), lambda n: (0, n, 0))] * 2,
        out_specs=[pl.BlockSpec((step, slots, features), lambda n: (n, 0, 0))] * 2,
        scratch_shapes=[pltpu.SMEM((slots,), jnp.int32), pltpu.SMEM((slots,), jnp.int32)],
    )(item_counts, lengths, lo, grad)

    small = small.reshape(-1)
    cuts = [features, features, wide, features, features, features]
    vectors, start = [], 0
    for cut in cuts:
        vectors.append(small[start : start + cut])
        start += cut
    gain_one_grad, shift_one_grad, bias_in_grad, bias_out_grad, gain_two_grad, shift_two_grad = vectors
    return (
        layer_out, input_grad, gain_one_grad, shift_one_grad, wi_grad, bias_in_grad, wo_grad, bias_out_grad, gain_two_grad, shift_two_grad,
    )


def solution(mesh):
    placed = (
        P("seq", "dp", None), P("dp"), P("dp"), P(), P(), P(), P(), P(), P(), P(), P(), P("seq", "dp", None),
    )
    wide = P("seq", "dp", None)
    return jax.shard_map(
        per_device,
        mesh=mesh,
        in_specs=placed,
        out_specs=(wide, wide, P(), P(), P(), P(), P(), P(), P(), P()),
        check_vma=False,
    )
```

time: 760 us -> 234 us (0.31); the launches traced: 751 us -> 233 us
  waiting for transfers between devices: 298 us -> 0 us
  Pallas kernels: 0 us -> 224 us
  blocking collectives: 163 us -> 0 us
  matrix products: 161 us -> 0 us
  local copies, waits for them, and re-layouts: 60.4 us -> 7.55 us
  other arithmetic: 36.8 us -> 0 us
  starting transfers between devices: 16.4 us -> 0 us
  between operations: 15.3 us -> 1.32 us
    reduce_scatter x2 -> x0, waiting for transfers between devices: 267 us -> none  [the longest x1 140 us: per_device(): lax.psum_scatter(grad_weight_out, ('dp', 'seq'), scatter_dimension=0, til...]
    pallas_call x0 -> x4, Pallas kernels: none -> 224 us  [the longest x1 144 us: per_device(): pl.pallas_call(functools.partial(backward_kernel, (sizes, far_slots, slot...]
    dot_general x14 -> x0, matrix products: 161 us -> none  [the longest x1 37.3 us: dense_forward(): jnp.dot(normed, weight_in, preferred_element_type=jnp.float32) + bias_in]
    unnamed x2 -> x0, blocking collectives: 107 us -> none
    all_to_all x2 -> x0, blocking collectives: 56.5 us -> none  [the longest x1 29.3 us: spectral(): lax.all_to_all(columns, 'seq', split_axis=0, concat_axis=2, tiled=True)]
    all_to_all x4 -> x0, waiting for transfers between devices: 31.2 us -> none  [the longest x1 12.5 us: spectral(): lax.all_to_all(sin_part, 'seq', split_axis=2, concat_axis=0, tiled=True)]
    convert_element_type x12 -> x0, other arithmetic: 26.6 us -> none  [the longest x1 7.37 us: per_device(): lax.all_gather(shares[2].astype(jnp.bfloat16), ('dp', 'seq'), axis=0, til...]
    all_to_all x6 -> x0, local copies, waits for them, and re-layouts: 16.6 us -> none  [the longest x1 4.4 us: spectral(): lax.all_to_all(columns, 'seq', split_axis=0, concat_axis=2, tiled=True)]
  transfers between devices with their start and end apart: 8 -> 0, of which waited for: 5 -> 0; matrix products, arithmetic and copies ran while one was open for 17% -> 0% of each run, Pallas kernels for 0% -> 0%
where the time goes in v2:
time: 234 us; the launch traced here: 233 us
  Pallas kernels  224 us (96%)
  local copies, waits for them, and re-layouts  7.55 us (3%)
    pallas_call x1, Pallas kernels, per_device(): pl.pallas_call(functools.partial(backward_kernel, (sizes, far_slots, slot...  144 us
    pallas_call x1, Pallas kernels, per_device(): pl.pallas_call(functools.partial(forward_kernel, (sizes, far_slots, slots...  58.7 us
    pallas_call x1, Pallas kernels, per_device(): pl.pallas_call(widen_kernel, name='widen', grid=(chunks,), out_shape=(sha...  12.5 us
    pallas_call x1, Pallas kernels, per_device(): pl.pallas_call(functools.partial(restore_kernel, slots), name='restore',...  8.82 us
    reshape x5, local copies, waits for them, and re-layouts, per_device(): vec = lambda v: v.reshape(1, -1)  6.33 us

profile of v2, /device:TPU:0, one launch (start us, length us, event | category | flops | bytes accessed | tf_op | source)
XLA Modules:
  0.0 232.6 jit_solution(9658597468499200013)
XLA Ops:
  1.3 1.3 reshape.52.refs_2_
  2.6 1.3 reshape.53.refs_3_
  3.8 1.3 reshape.55.refs_5_
  5.1 1.3 reshape.56.refs_6_
  6.4 1.3 reshape.57.refs_7_
  7.6 58.7 %forward.1 = (bf16[12,1024,256]{2,1,0:T(8,128)(2,1)}, bf16[12,1024,256]{2,1,0:T(8,128)(2,1)}, bf16[1024,768]{1,0:T(8,128)(2,1)}, f32[1024,768]{1,0:T(8,128)}, f3...) custom-call(s32[1]{0:T(128)S(6)} %copy.24.refs_0_.count_ref, s32[8]{0:T(128)} %length_ref.1, ...), custom_call_target="tpu_custom_call" | custom-call | tf_op jit(solution)/shard_map/forward/pallas_call | solution.py:699
  66.4 143.7 %backward.1 = (bf16[12,3072,128]{2,1,0:T(8,128)(2,1)}, f32[1024,768]{1,0:T(8,128)}, f32[64,128]{1,0:T(8,128)}) custom-call(s32[1]{0:T(128)S(6)} %copy.24.refs_0_.count_ref, s32[8]{0:T(128)} %length_ref.1, f32[1,768]{1,0:T(1,128)} %reshape.52.refs_2_, f32[24,768]{1,0:T(8,128)} %get-tuple-element.25.refs_3_, bf16[12,1024,256]{2,1,0:T(8,128)(2,1)} %get-tuple-element.26.refs_4_, ...), custom_call_target="tpu_custom_call" | custom-call | tf_op jit(solution)/shard_map/backward/pallas_call | solution.py:743
  210.1 0.0 copy-start
  210.1 8.8 %restore.1 = (f32[128,8,768]{2,1,0:T(8,128)}, f32[128,8,768]{2,1,0:T(8,128)}) custom-call(s32[1]{0:T(128)S(6)} %copy.24.refs_0_.count_ref, s32[8]{0:T(128)} %length_ref.1, f32[8,128,768]{2,1,0:T(8,128)} %bitcast.15, f32[8,128,768]{2,1,0:T(8,128)} %bitcast.16), custom_call_target="tpu_custom_call" | custom-call | tf_op jit(solution)/shard_map/restore/pallas_call | solution.py:813
  218.9 0.0 copy-done
  218.9 0.6 slice_bitcast_fusion
  219.5 0.6 slice_bitcast_fusion.1
  220.1 12.5 %widen.1 = (f32[768,3072]{1,0:T(8,128)}, f32[3072,768]{1,0:T(8,128)}) custom-call(bf16[12,3072,128]{2,1,0:T(8,128)(2,1)} %get-tuple-element.35.full_ref), custom_call_target="tpu_custom_call" | custom-call | tf_op jit(solution)/shard_map/widen/pallas_call | solution.py:799
Async XLA Ops:
  210.1 8.8 %copy-start = (f32[64,128]{1,0:T(8,128)S(1)}, f32[64,128]{1,0:T(8,128)}, u32[]{:S(2)}) copy-start(f32[64,128]{1,0:T(8,128)} %get-tuple-element.34) | copy-start | bytes 98308

commit v3 on v2

v3 whole, which is shorter than its diff:
```python
import functools
import math

import jax
import jax.numpy as jnp
import numpy as np
from jax import lax
from jax.experimental import pallas as pl
from jax.experimental.pallas import tpu as pltpu
from jax.sharding import PartitionSpec as P

EPSILON = 1e-05
MESH = pl.DeviceIdType.MESH
LANES = 128
WIDE = 512
BF16 = jnp.bfloat16
F32 = jnp.float32


def dft_tables(count):
    index = np.arange(count, dtype=np.int64)
    turns = (index[:, None] * index[None, :] % count).astype(np.float32)
    angle = (turns * np.float32(2.0 * math.pi / count)).astype(np.float64)
    return np.cos(angle).astype(np.float32), np.sin(angle).astype(np.float32)


def aligned(value, step):
    return pl.multiple_of(value, step)


def bit_of(value, k):
    return (value // k) % 2


def flipped(value, k):
    return value + k * (1 - 2 * bit_of(value, k))


def axis_bits(axis, size):
    return [(axis, 1 << b) for b in range(size.bit_length() - 1)]


class Cube:
    def __init__(self, sizes, mids):
        dp, seq = sizes
        bits = axis_bits(1, seq) + axis_bits(0, dp)
        first, near, rest = bits[:1], bits[1:4], bits[4:]
        self.orders = [first + [near[i] for i in mid] + rest for mid in mids]
        self.bits = bits
        self.stages = len(bits)
        self.me = (lax.axis_index("dp"), lax.axis_index("seq"))
        self.values = {bit: self.value(bit) for bit in bits}
        self.partners = {bit: self.partner(bit) for bit in bits}

    def value(self, bit):
        return bit_of(self.me[bit[0]], bit[1])

    def partner(self, bit):
        axis, k = bit
        other = flipped(self.me[axis], k)
        return (other, self.me[1]) if axis == 0 else (self.me[0], other)

    def offset(self, order, level, rows):
        total = 0
        for s in range(level):
            total = total + self.values[self.orders[order][s]] * (rows >> (s + 1))
        return total


class Exchange:
    def __init__(self, size, rows, buf, send, recv):
        self.size, self.rows, self.buf, self.send_sem, self.recv_sem = size, rows, buf, send, recv
        self.dp, self.q = lax.axis_index("dp"), lax.axis_index("seq")
        self.order = [1 << b for b in reversed(range(size.bit_length() - 1))]

    def owner(self, pattern):
        index = self.q
        for k in self.order:
            if pattern & k:
                index = flipped(index, k)
        return index

    def copy(self, slot, pattern):
        hop = pattern & -pattern
        place = pl.ds(aligned(self.owner(pattern - hop) * self.rows, self.rows), self.rows)
        ref = self.buf.at[slot, place]
        return pltpu.make_async_remote_copy(
            src_ref=ref,
            dst_ref=ref,
            send_sem=self.send_sem.at[slot, pattern],
            recv_sem=self.recv_sem.at[slot, pattern],
            device_id=(self.dp, flipped(self.q, hop)),
            device_id_type=MESH,
        )

    def patterns(self, far):
        return range(1, self.size) if far else range(1, 2)

    def start_own(self, slot, far):
        for pattern in self.patterns(far):
            if pattern & (pattern - 1) == 0:
                self.copy(slot, pattern).start()

    def forward(self, slot):
        for pattern in self.patterns(True):
            if pattern & 1 == 0:
                self.copy(slot, pattern).wait_recv()
                for k in self.order:
                    if k < (pattern & -pattern):
                        self.copy(slot, pattern | k).start()

    def wait_near(self, slot, far):
        for pattern in self.patterns(far):
            if pattern & 1:
                self.copy(slot, pattern).wait_recv()

    def wait_sends(self, slot, far):
        for pattern in self.patterns(far):
            self.copy(slot, pattern).wait_send()


def greet(partners):
    barrier = pltpu.get_barrier_semaphore()
    for partner in partners:
        pl.semaphore_signal(barrier, inc=1, device_id=partner, device_id_type=MESH)
    pl.semaphore_wait(barrier, len(partners))


def rank_slots(count_ref, length_ref, perm_s, slen_s, slots):
    count = count_ref[0]
    live = [jnp.where(i < count, length_ref[i], 0) for i in range(slots)]
    ranks = []
    for i in range(slots):
        rank = 0
        for k in range(slots):
            if k != i:
                ahead = live[k] >= live[i] if k < i else live[k] > live[i]
                rank = rank + jnp.where(ahead, 1, 0)
        ranks.append(rank)
    for j in range(slots):
        perm, length = 0, 0
        for i in range(slots):
            here = ranks[i] == j
            perm = perm + jnp.where(here, i, 0)
            length = length + jnp.where(here, live[i], 0)
        perm_s[j] = perm
        slen_s[j] = length


def live_rows(slen_s, slot, first, rows):
    position = first + lax.broadcasted_iota(jnp.int32, (rows, 1), 0)
    return position < slen_s[slot]


def fold8(values):
    rows, lanes = values.shape
    return values.reshape(rows // 8, 8, lanes).sum(axis=0)


def normalize(values):
    center = values - jnp.mean(values, axis=-1, keepdims=True)
    spread = jnp.mean(center * center, axis=-1, keepdims=True)
    inverse = lax.rsqrt(spread + EPSILON)
    return center * inverse, inverse


def norm_back(grad_hat, normal, inverse):
    first = jnp.mean(grad_hat, axis=-1, keepdims=True)
    second = jnp.mean(grad_hat * normal, axis=-1, keepdims=True)
    return inverse * (grad_hat - first - normal * second)


def mix_slot(slot, far, exchange, tables, buf, uv, place):
    rows = exchange.rows
    if far:
        table, block = tables[...], buf[slot]
    else:
        base = aligned(exchange.q // 2 * (2 * rows), 2 * rows)
        table, block = tables[:, pl.ds(base, 2 * rows)], buf[slot, pl.ds(base, 2 * rows), :]
    both = jnp.dot(table, block, preferred_element_type=F32).astype(BF16)
    width = both.shape[1]
    uv[pl.ds(place, rows), :width] = both[:rows]
    uv[pl.ds(place, rows), width:] = both[rows:]


def group_at(i, near_groups, count):
    if near_groups == 0:
        return count - 1 - i
    return jnp.where(i < near_groups, count - near_groups + i, count - 1 - i)


def forward_kernel(cfg, *refs):
    sizes, far_slots, slots, group = cfg
    (
        count_ref, length_ref, vec_ref, x_hbm, cot_hbm, wi_hbm, wo_hbm, sc_hbm, hc_hbm,
        act_o, dg_o, nrm_o, sum_o, gs_o, gb_o, lo_o, part_o,
        perm_s, slen_s, x_v, cot_v, wi_v, wo_v, sc_v, hc_v, buf, uv, sum_v, nrm_v, act_v, dg_v, gs_v, gb_v, lo_v, br_v,
        load_sem, out_sem, send_sem, recv_sem,
    ) = refs
    rows, _, features = x_v.shape
    wide = wi_v.shape[1]
    seq_total = rows * sizes[1]
    scale = 1.0 / math.sqrt(features * seq_total)
    exchange = Exchange(sizes[1], rows, buf, send_sem, recv_sem)
    q = exchange.q
    first = q * rows
    gain_one, shift_one, bias_out, gain_two, shift_two = (lambda i=i: vec_ref[i : i + 1, :] for i in range(5))
    loads = [
        pltpu.make_async_copy(x_hbm, x_v, load_sem.at[0]),
        pltpu.make_async_copy(sc_hbm.at[q], sc_v, load_sem.at[1]),
        pltpu.make_async_copy(hc_hbm, hc_v, load_sem.at[2]),
        pltpu.make_async_copy(wi_hbm, wi_v, load_sem.at[3]),
        pltpu.make_async_copy(wo_hbm, wo_v, load_sem.at[4]),
        pltpu.make_async_copy(cot_hbm, cot_v, load_sem.at[5]),
    ]
    loads[0].start()
    rank_slots(count_ref, length_ref, perm_s, slen_s, slots)
    greet([(exchange.dp, flipped(q, k)) for k in exchange.order])
    loads[0].wait()
    for load in loads[1:]:
        load.start()

    def prepare(i, _):
        slot = jnp.where(i < far_slots, far_slots - 1 - i, i) if far_slots < slots else slots - 1 - i
        value = jnp.where(live_rows(slen_s, slot, first, rows), x_v[:, perm_s[slot], :], 0.0)
        sum_v[pl.ds(aligned(slot * rows, rows), rows), :] = value
        buf[slot, pl.ds(aligned(first, rows), rows), :] = value.astype(BF16)
        pl.when(i < far_slots)(lambda: exchange.start_own(slot, True))
        if far_slots < slots:
            pl.when(i >= far_slots)(lambda: exchange.start_own(slot, False))
        return 0

    lax.fori_loop(0, slots, prepare, 0)
    part_o[...] = jnp.zeros_like(part_o)
    for load in loads[1:3]:
        load.wait()

    batch = group * rows
    span = features
    count = slots // group
    near_groups = (slots - far_slots) // group

    def outs(base):
        place = pl.ds(base, batch)
        copies = [
            pltpu.make_async_copy(nrm_v.at[place], nrm_o.at[place], out_sem.at[0]),
            pltpu.make_async_copy(sum_v.at[place], sum_o.at[place], out_sem.at[1]),
            pltpu.make_async_copy(gs_v.at[place], gs_o.at[place], out_sem.at[2]),
            pltpu.make_async_copy(lo_v.at[place], lo_o.at[place], out_sem.at[3]),
            pltpu.make_async_copy(gb_v.at[place], gb_o.at[place], out_sem.at[6]),
        ]
        for n in range(wide // WIDE):
            cut = pl.ds(n * WIDE, WIDE)
            copies.append(pltpu.make_async_copy(act_v.at[place, cut], act_o.at[n, place], out_sem.at[4]))
            copies.append(pltpu.make_async_copy(dg_v.at[place, cut], dg_o.at[n, place], out_sem.at[5]))
        return copies

    def bring(slot0):
        for k in reversed(range(group)):
            exchange.forward(slot0 + k)

    def mixing(slot0, far):
        for k in reversed(range(group)):
            exchange.wait_near(slot0 + k, far)
            mix_slot(slot0 + k, far, exchange, sc_v, buf, uv, k * rows)

    def work(i, _):
        slot0 = group_at(i, near_groups, count) * group
        base = aligned(slot0 * rows, batch)
        place = pl.ds(base, batch)
        if near_groups < count:
            pl.when(i >= near_groups)(lambda: mixing(slot0, True))
        if near_groups > 0:
            pl.when(i < near_groups)(lambda: mixing(slot0, False))
        mixed = jnp.dot(uv[...], hc_v[...], preferred_element_type=F32)
        sum_v[place, :] = sum_v[place, :] + (mixed * scale).astype(BF16).astype(F32)

        def norm_one(k, _):
            here = pl.ds(aligned(base + k * rows, rows), rows)
            hat, _ = normalize(sum_v[here, :])
            nrm_v[here, :] = (hat * gain_one() + shift_one()).astype(BF16)
            return 0

        lax.fori_loop(0, group, norm_one, 0)

        @pl.when(i == 0)
        def _():
            for load in loads[3:]:
                load.wait()

        def expand(n, _):
            cut = pl.ds(aligned(n * span, span), span)
            hidden = jnp.dot(nrm_v[place, :], wi_v[:, cut], preferred_element_type=F32) + vec_ref[pl.ds(5 + n, 1), :]
            gate = 0.5 + 0.5 * lax.erf(hidden * math.sqrt(0.5))
            slope = gate + hidden * (jnp.exp(hidden * hidden * -0.5) * (1.0 / math.sqrt(2.0 * math.pi)))
            act_v[place, cut] = (hidden * gate).astype(BF16)
            dg_v[place, cut] = slope.astype(BF16)
            return 0

        lax.fori_loop(0, wide // span, expand, 0)
        br_v[...] = jnp.dot(act_v[place, :], wo_v[...], preferred_element_type=F32)

        def norm_two(k, _):
            here = pl.ds(aligned(base + k * rows, rows), rows)
            local = pl.ds(aligned(k * rows, rows), rows)
            slot = slot0 + k
            live = live_rows(slen_s, slot, first, rows)
            hat, inverse = normalize(sum_v[here, :] + (br_v[local, :] + bias_out()))
            grad = jnp.where(live, cot_v[:, perm_s[slot], :], 0.0)
            lo_v[here, :] = jnp.where(live, hat * gain_two() + shift_two(), 0.0)
            part_o[0:8, :] = part_o[0:8, :] + fold8(grad * hat)
            part_o[8:16, :] = part_o[8:16, :] + fold8(grad)
            second = norm_back(grad * gain_two(), hat, inverse)
            low = second.astype(BF16)
            gs_v[here, :] = second
            gb_v[here, :] = low
            part_o[16:24, :] = part_o[16:24, :] + fold8(low.astype(F32))
            return 0

        lax.fori_loop(0, group, norm_two, 0)
        for copy in outs(base):
            copy.start()
        if near_groups < count:

            @pl.when((i + 1 >= near_groups) & (i + 1 < count))
            def _():
                bring(group_at(i + 1, near_groups, count) * group)

        return 0

    if near_groups == 0:
        bring((count - 1) * group)
    lax.fori_loop(0, count, work, 0)

    def finish(slot, _):
        pl.when(slot < far_slots)(lambda: exchange.wait_sends(slot, True))
        if far_slots < slots:
            pl.when(slot >= far_slots)(lambda: exchange.wait_sends(slot, False))
        return 0

    lax.fori_loop(0, slots, finish, 0)

    def flush(g, _):
        for copy in outs(aligned(g * batch, batch)):
            copy.wait()
        return 0

    lax.fori_loop(0, count, flush, 0)


def backward_kernel(cfg, *refs):
    sizes, far_slots, slots, group, parts, mids, lags, plan = cfg
    cube = Cube(sizes, mids)
    S = cube.stages
    (
        count_ref, length_ref, vec_ref, part_ref,
        act_hbm, dg_hbm, nrm_hbm, sum_hbm, gs_hbm, gb_hbm, wi_hbm, wo_hbm, sc_hbm, hc_hbm,
        full_o, ig_o, small_o,
        perm_s, slen_s, gs_v, sum_v, nrm_v, gb_v, gh_v, gn_v, act_v, dg_v, wi_v, wo_v, sc_v, hc_v, buf, uv, ig_v,
        bin_v, one_v, small_v, part_v, full,
    ) = refs[:39]
    landed = refs[39 : 39 + S]
    (
        small_recv, load_sem, sum_sem, stream_sem, out_sem, ig_sem, send_sem, recv_sem,
        rs_s, rs_r, ag_s, ag_r, sm_s, sm_r,
    ) = refs[39 + S :]
    ticks, tick_rows, _ = part_v.shape
    message = tick_rows // parts
    chunks = act_hbm.shape[0]
    per_tick = chunks // ticks
    features = nrm_v.shape[1]
    rows = gs_v.shape[0] // slots
    batch = group * rows
    scale = 1.0 / math.sqrt(features * rows * sizes[1])
    exchange = Exchange(sizes[1], rows, buf, send_sem, recv_sem)
    q = exchange.q
    first = q * rows
    loads = [
        pltpu.make_async_copy(gb_hbm, gb_v, load_sem.at[0]),
        pltpu.make_async_copy(nrm_hbm, nrm_v, load_sem.at[1]),
        pltpu.make_async_copy(gs_hbm, gs_v, load_sem.at[2]),
        pltpu.make_async_copy(sc_hbm.at[q], sc_v, load_sem.at[3]),
        pltpu.make_async_copy(hc_hbm, hc_v, load_sem.at[4]),
    ]

    def turn(i):
        return jnp.where(i < far_slots, far_slots - 1 - i, i) if far_slots < slots else slots - 1 - i

    def sum_copy(i):
        place = pl.ds(aligned(turn(i) * rows, rows), rows)
        return pltpu.make_async_copy(sum_hbm.at[place], sum_v.at[lax.rem(i, 2)], sum_sem.at[lax.rem(i, 2)])

    def streams(n, slot):
        cut = pl.ds(aligned(n * WIDE, WIDE), WIDE)
        return [
            pltpu.make_async_copy(act_hbm.at[n], act_v.at[slot], stream_sem.at[0, slot]),
            pltpu.make_async_copy(wo_hbm.at[cut], wo_v.at[slot], stream_sem.at[1, slot]),
            pltpu.make_async_copy(dg_hbm.at[n], dg_v.at[slot], stream_sem.at[2, slot]),
            pltpu.make_async_copy(wi_hbm.at[:, cut], wi_v.at[slot], stream_sem.at[3, slot]),
        ]

    loads[0].start()
    for copy in streams(0, 0):
        copy.start()
    for load in loads[1:]:
        load.start()
    for i in range(2):
        sum_copy(i).start()
    rank_slots(count_ref, length_ref, perm_s, slen_s, slots)
    greet([cube.partner(bit) for bit in cube.bits])

    starts = [[j * message + cube.offset(j, level, message) for level in range(S + 1)] for j in range(parts)]

    def rs(m, t, j, s):
        bit = cube.orders[j][s]
        half = message >> (s + 1)
        off = starts[j][s] + (1 - cube.values[bit]) * half
        return pltpu.make_async_remote_copy(
            src_ref=part_v.at[t, pl.ds(aligned(off, 16), half)],
            dst_ref=landed[s].at[m],
            send_sem=rs_s.at[s],
            recv_sem=rs_r.at[s, m],
            device_id=cube.partners[bit],
            device_id_type=MESH,
        )

    def ag(m, t, j, s):
        bit = cube.orders[j][s]
        half = message >> (s + 1)
        ref = full.at[t, pl.ds(aligned(starts[j][s + 1], 16), half)]
        return pltpu.make_async_remote_copy(
            src_ref=ref,
            dst_ref=ref,
            send_sem=ag_s.at[s],
            recv_sem=ag_r.at[s, m],
            device_id=cube.partners[bit],
            device_id_type=MESH,
        )

    def add(m, t, j, s):
        half = message >> (s + 1)
        place = pl.ds(aligned(starts[j][s + 1], 16), half)
        total = part_v[t, place, :].astype(F32) + landed[s][m].astype(F32)
        target = full if s == S - 1 else part_v
        target[t, place, :] = total.astype(BF16)

    def out(t, j):
        place = pl.ds(j * message, message)
        return pltpu.make_async_copy(full.at[t, place], full_o.at[t, place], out_sem.at[t, j])

    def event(k, m, t, j):
        if k == 0:
            rs(m, t, j, 0).start()
        elif k <= S:
            rs(m, t, j, k - 1).wait_recv()
            add(m, t, j, k - 1)
            (rs(m, t, j, k) if k < S else ag(m, t, j, S - 1)).start()
        elif k < 2 * S:
            s = 2 * S - k
            ag(m, t, j, s).wait_recv()
            ag(m, t, j, s - 1).start()
        else:
            ag(m, t, j, 0).wait_recv()
            out(t, j).start()

    def sends_done():
        for s in range(S):
            for sem in (rs_s.at[s], ag_s.at[s]):
                pltpu.make_async_copy(landed[s], landed[s], sem).wait()

    when = [0 if per_tick == 1 and parts == 4 else parts]
    for lag in lags:
        when.append(when[-1] + lag)

    def events(tick, j):
        for k in reversed(range(2 * S + 1)):
            t = tick + (j - when[k]) // parts
            jj = (j - when[k]) % parts
            pl.when((t >= 0) & (t < ticks))(functools.partial(event, k, t * parts + jj, t, jj))

    bin_v[...] = jnp.zeros_like(bin_v)
    one_v[...] = jnp.zeros_like(one_v)
    gn_v[...] = jnp.zeros_like(gn_v)
    small_v[...] = jnp.zeros_like(small_v)
    loads[0].wait()

    def contract(left, right, dims):
        return lax.dot_general(left, right, ((dims, dims), ((), ())), preferred_element_type=F32)

    def weigh_out(n, slot, t, base):
        streams(n, slot)[0].wait()
        grad = contract(act_v[slot], gb_v[...], (0,)).astype(BF16)
        for i in range(features // LANES):
            part_v[t, pl.ds(base + i * WIDE, WIDE), :] = grad[:, i * LANES : (i + 1) * LANES]

    def pull(n, slot, t, base):
        streams(n, slot)[1].wait()
        streams(n, slot)[2].wait()
        pulled = contract(gb_v[...], wo_v[slot], (1,)) * dg_v[slot].astype(F32)
        pulled = pulled.astype(BF16)
        gh_v[...] = pulled
        bin_v[n] = fold8(pulled.astype(F32))

    def weigh_in(n, slot, t, base):
        pl.when(n == 0)(loads[1].wait)
        grad = contract(nrm_v[...], gh_v[...], (0,)).astype(BF16)
        for i in range(WIDE // LANES):
            place = pl.ds(base + features // LANES * WIDE + i * features, features)
            part_v[t, place, :] = grad[:, i * LANES : (i + 1) * LANES]

    def spread(n, slot, t, base):
        streams(n, slot)[3].wait()
        for i in range(2):
            here = pl.ds(i * (slots // 2) * rows, slots // 2 * rows)
            gn_v[here, :] = gn_v[here, :] + contract(gh_v[here, :], wi_v[slot], (1,))

    steps = [weigh_out, pull, weigh_in, spread]

    def compute(tick, j):
        if per_tick == 1 and parts == 4:
            slot = lax.rem(tick, 2)
            if j == 0:
                for copy in streams(tick + 1, 1 - slot):
                    pl.when(tick + 1 < chunks)(copy.start)
            steps[j](tick, slot, tick, 0)
        elif j == 0:

            def whole(u, _):
                n = tick * per_tick + u
                slot = lax.rem(n, 2)
                for copy in streams(n + 1, 1 - slot):
                    pl.when(n + 1 < chunks)(copy.start)
                for step in steps:
                    step(n, slot, tick, aligned(u * (tick_rows // per_tick), LANES))
                return 0

            lax.fori_loop(0, per_tick, whole, 0)

    def back(i, _):
        slot = turn(i)
        here = pl.ds(aligned(slot * rows, rows), rows)
        pl.when(i == 0)(loads[2].wait)
        sum_copy(i).wait()
        hat, inverse = normalize(sum_v[lax.rem(i, 2)])
        grad = gn_v[here, :]
        one_v[0:8, :] = one_v[0:8, :] + fold8(grad * hat)
        one_v[8:16, :] = one_v[8:16, :] + fold8(grad)
        grad = gs_v[here, :] + norm_back(grad * vec_ref[0:1, :], hat, inverse)
        gs_v[here, :] = grad
        buf[slot, pl.ds(aligned(first, rows), rows), :] = grad.astype(BF16)
        pl.when(i < far_slots)(lambda: exchange.start_own(slot, True))
        if far_slots < slots:
            pl.when(i >= far_slots)(lambda: exchange.start_own(slot, False))
        pl.when(i + 2 < slots)(lambda: sum_copy(i + 2).start())
        return 0

    def small_copy(s):
        return pltpu.make_async_remote_copy(
            src_ref=small_v.at[s],
            dst_ref=small_recv.at[s],
            send_sem=sm_s.at[s],
            recv_sem=sm_r.at[s],
            device_id=cube.partners[cube.bits[s]],
            device_id_type=MESH,
        )

    def small_start():
        row = 0
        vectors = [one_v[0:8, :], one_v[8:16, :]] + [bin_v[n] for n in range(chunks)]
        vectors += [part_ref[16:24, :], part_ref[0:8, :], part_ref[8:16, :]]
        for vector in vectors:
            vector = jnp.sum(vector, axis=0, keepdims=True)
            for i in range(vector.shape[1] // LANES):
                small_v[0, row : row + 1, :] = vector[:, i * LANES : (i + 1) * LANES]
                row += 1
        small_copy(0).start()

    def small_step(s):
        small_copy(s).wait()
        if s + 1 < S:
            small_v[s + 1] = small_v[s] + small_recv[s]
            small_copy(s + 1).start()
        else:
            small_o[...] = small_v[s] + small_recv[s]

    count = slots // group
    near_groups = (slots - far_slots) // group

    def grad_copy(i):
        base = aligned(group_at(i, near_groups, count) * batch, batch)
        return pltpu.make_async_copy(ig_v.at[lax.rem(i, 2)], ig_o.at[pl.ds(base, batch)], ig_sem.at[lax.rem(i, 2)])

    def mixing(i, k, far):
        slot = group_at(i, near_groups, count) * group + k
        exchange.wait_near(slot, far)
        mix_slot(slot, far, exchange, sc_v, buf, uv, k * rows)

    def hidden_mix(i):
        pl.when(i >= 2)(lambda: grad_copy(i - 2).wait())
        ig_v[lax.rem(i, 2)] = jnp.dot(uv[...], hc_v[...], preferred_element_type=F32)

    def finish(i):
        for k in range(group):
            slot = group_at(i, near_groups, count) * group + k
            here = pl.ds(aligned(slot * rows, rows), rows)
            local = pl.ds(k * rows, rows)
            grad = gs_v[here, :] + ig_v[lax.rem(i, 2), local, :] * scale
            ig_v[lax.rem(i, 2), local, :] = jnp.where(live_rows(slen_s, slot, first, rows), grad, 0.0)
        grad_copy(i).start()

    def bring(i):
        for k in reversed(range(group)):
            exchange.forward(group_at(i, near_groups, count) * group + k)

    small_at, near_at, far_at, lead = plan

    def drain(tick, j):
        d = tick - ticks

        @pl.when(d == 0)
        def _():
            share = -(-slots // parts)
            lax.fori_loop(min(j * share, slots), min((j + 1) * share, slots), back, 0)

        here = lambda at: pl.when(d * parts + j == at)
        if j == small_at % parts:
            here(small_at)(small_start)
        for s in range(S):
            at = small_at + 3 * (s + 1)
            if j == at % parts:
                here(at)(functools.partial(small_step, s))
        if j == 0:

            @pl.when(d == 1)
            def _():
                for load in loads[3:]:
                    load.wait()

        for far, start, low, high in ((False, near_at, 0, near_groups), (True, far_at, near_groups, count)):
            if low == high:
                continue
            i = d - start + low

            @pl.when((i >= low) & (i < high))
            def _():
                subs = [
                    lambda: mixing(i, 0, far),
                    lambda: [mixing(i, k, far) for k in range(1, group)],
                    lambda: hidden_mix(i),
                    lambda: finish(i),
                ]
                for at, sub in enumerate(subs):
                    if min(at, parts - 1) == j:
                        sub()

            if far and j == parts - 1:
                ahead = i + lead
                pl.when((ahead >= low) & (ahead < high))(lambda: bring(ahead))

    last = ticks + max(
        -(-(when[-1] + 1) // parts),
        (small_at + 3 * S) // parts + 1,
        near_at + near_groups,
        far_at + count - near_groups,
    )

    def body(tick, _):
        for j in range(parts):
            pl.when(tick < ticks)(lambda: compute(tick, j))
            events(tick, j)
            pl.when(tick >= ticks)(lambda: drain(tick, j))
        return 0

    lax.fori_loop(0, last, body, 0)

    def settle(slot, _):
        pl.when(slot < far_slots)(lambda: exchange.wait_sends(slot, True))
        if far_slots < slots:
            pl.when(slot >= far_slots)(lambda: exchange.wait_sends(slot, False))
        return 0

    lax.fori_loop(0, slots, settle, 0)
    for i in range(max(0, count - 2), count):
        grad_copy(i).wait()

    def finish_out(t, _):
        for j in range(parts):
            out(t, j).wait()
        return 0

    lax.fori_loop(0, ticks, finish_out, 0)
    sends_done()


def widen_kernel(full_ref, wi_ref, wo_ref):
    features = wi_ref.shape[0]
    for u in range(full_ref.shape[0]):
        for i in range(features // LANES):
            place = slice(u * WIDE, (u + 1) * WIDE)
            wo_ref[place, i * LANES : (i + 1) * LANES] = full_ref[u, pl.ds(i * WIDE, WIDE), :].astype(F32)
        for i in range(WIDE // LANES):
            start = features // LANES * WIDE + i * features
            place = slice(u * WIDE + i * LANES, u * WIDE + (i + 1) * LANES)
            wi_ref[:, place] = full_ref[u, pl.ds(start, features), :].astype(F32)


def restore_kernel(slots, count_ref, length_ref, lo_ref, ig_ref, lo_out, ig_out, perm_s, slen_s):
    rank_slots(count_ref, length_ref, perm_s, slen_s, slots)
    for j in range(slots):
        lo_out[:, perm_s[j], :] = lo_ref[j]
        ig_out[:, perm_s[j], :] = ig_ref[j]


ANY = pl.BlockSpec(memory_space=pl.ANY)
SMEM = pl.BlockSpec(memory_space=pltpu.SMEM)
VMEM = pl.BlockSpec(memory_space=pltpu.VMEM)
DMA = pltpu.SemaphoreType.DMA
LAGS = [4, 4, 4, 4, 4, 4, 4, 4, 4, 4]
PLAN = (4, 1, 4, 1)
FAR_PLAN = (4, 1, 4, 1)
MIDS = ((0, 1, 2), (1, 0, 2), (2, 0, 1), (1, 2, 0))
FAR_MIDS = ((1, 2, 0), (2, 1, 0), (1, 0, 2), (2, 0, 1))


def run_forward(sizes, far_slots, slots, *operands, group=2, name="forward", cid=1):
    rows, _, features = operands[3].shape
    wide = operands[5].shape[1]
    seq_total = rows * sizes[1]
    flat, batch, chunks = rows * slots, group * rows, wide // WIDE
    shape = jax.ShapeDtypeStruct
    return pl.pallas_call(
        functools.partial(forward_kernel, (sizes, far_slots, slots, group)),
        name=name,
        out_shape=(
            shape((chunks, flat, WIDE), BF16),
            shape((chunks, flat, WIDE), BF16),
            shape((flat, features), BF16),
            shape((flat, features), F32),
            shape((flat, features), F32),
            shape((flat, features), BF16),
            shape((flat, features), F32),
            shape((24, features), F32),
        ),
        in_specs=[SMEM] * 2 + [VMEM] + [ANY] * 6,
        out_specs=[ANY] * 7 + [VMEM],
        scratch_shapes=[
            pltpu.SMEM((slots,), jnp.int32),
            pltpu.SMEM((slots,), jnp.int32),
            pltpu.VMEM((rows, slots, features), F32),
            pltpu.VMEM((rows, slots, features), F32),
            pltpu.VMEM((features, wide), BF16),
            pltpu.VMEM((wide, features), BF16),
            pltpu.VMEM((2 * rows, seq_total), BF16),
            pltpu.VMEM((2 * features, features), BF16),
            pltpu.VMEM((slots, seq_total, features), BF16),
            pltpu.VMEM((batch, 2 * features), BF16),
            pltpu.VMEM((flat, features), F32),
            pltpu.VMEM((flat, features), BF16),
            pltpu.VMEM((flat, wide), BF16),
            pltpu.VMEM((flat, wide), BF16),
            pltpu.VMEM((flat, features), F32),
            pltpu.VMEM((flat, features), BF16),
            pltpu.VMEM((flat, features), F32),
            pltpu.VMEM((batch, features), F32),
            DMA((6,)),
            DMA((7,)),
            DMA((slots, sizes[1])),
            DMA((slots, sizes[1])),
        ],
        compiler_params=pltpu.CompilerParams(collective_id=cid, has_side_effects=True, vmem_limit_bytes=62 << 20),
    )(*operands)


def run_backward(sizes, far_slots, slots, ticks, tick_rows, parts, *operands, group=2, mids=None, lags=None, plan=None, name="backward", cid=2):
    devices = sizes[0] * sizes[1]
    chunks, flat, _ = operands[4].shape
    features, wide = operands[10].shape
    rows = flat // slots
    seq_total = rows * sizes[1]
    batch = group * rows
    message = tick_rows // parts
    shape = jax.ShapeDtypeStruct
    mostly_far = far_slots > slots * 5 // 8
    mids = mids or (FAR_MIDS if mostly_far else MIDS)
    plan = plan or (FAR_PLAN if mostly_far else PLAN)
    lags = lags or LAGS
    stages = devices.bit_length() - 1
    lags = (lags[:stages] + [2] * stages)[:stages] + ([2] * stages + lags[-stages:])[-stages:]
    return pl.pallas_call(
        functools.partial(backward_kernel, (sizes, far_slots, slots, group, parts, mids, lags, plan)),
        name=name,
        out_shape=(
            shape((ticks, tick_rows, LANES), BF16),
            shape((flat, features), F32),
            shape((64, LANES), F32),
        ),
        in_specs=[SMEM] * 2 + [VMEM] * 2 + [ANY] * 10,
        out_specs=[ANY] * 2 + [VMEM],
        scratch_shapes=[
            pltpu.SMEM((slots,), jnp.int32),
            pltpu.SMEM((slots,), jnp.int32),
            pltpu.VMEM((flat, features), F32),
            pltpu.VMEM((2, rows, features), F32),
            pltpu.VMEM((flat, features), BF16),
            pltpu.VMEM((flat, features), BF16),
            pltpu.VMEM((flat, WIDE), BF16),
            pltpu.VMEM((flat, features), F32),
            pltpu.VMEM((2, flat, WIDE), BF16),
            pltpu.VMEM((2, flat, WIDE), BF16),
            pltpu.VMEM((2, features, WIDE), BF16),
            pltpu.VMEM((2, WIDE, features), BF16),
            pltpu.VMEM((2 * rows, seq_total), BF16),
            pltpu.VMEM((2 * features, features), BF16),
            pltpu.VMEM((slots, seq_total, features), BF16),
            pltpu.VMEM((batch, 2 * features), BF16),
            pltpu.VMEM((2, batch, features), F32),
            pltpu.VMEM((chunks, 8, WIDE), F32),
            pltpu.VMEM((16, features), F32),
            pltpu.VMEM((stages, 64, LANES), F32),
            pltpu.VMEM((ticks, tick_rows, LANES), BF16),
            pltpu.VMEM((ticks, tick_rows, LANES), BF16),
        ]
        + [pltpu.VMEM((ticks * parts, message >> (s + 1), LANES), BF16) for s in range(stages)]
        + [
            pltpu.VMEM((stages, 64, LANES), F32),
            DMA((5,)),
            DMA((2,)),
            DMA((4, 2)),
            DMA((ticks, parts)),
            DMA((2,)),
            DMA((slots, sizes[1])),
            DMA((slots, sizes[1])),
            DMA((stages,)),
            DMA((stages, ticks * parts)),
            DMA((stages,)),
            DMA((stages, ticks * parts)),
            DMA((stages,)),
            DMA((stages,)),
        ],
        compiler_params=pltpu.CompilerParams(collective_id=cid, has_side_effects=True, vmem_limit_bytes=62 << 20),
    )(*operands)


def cut_messages(devices, chunks, chunk_rows):
    per_tick, parts = min(
        (count, -cut)
        for count in range(1, chunks + 1)
        for cut in range(1, 5)
        if chunks % count == 0 and chunk_rows * count % (devices * 16 * cut) == 0
    )
    return per_tick, -parts


def layer(far_slots, index, sizes, inputs, item_counts, lengths, vectors, weight_in, weight_out, cotangent, seq_table, hid_table):
    rows, slots, features = inputs.shape
    wide = weight_in.shape[1]
    chunks = wide // WIDE
    chunk_rows = 2 * features * WIDE // LANES
    per_tick, parts = cut_messages(sizes[0] * sizes[1], chunks, chunk_rows)
    act, dg, nrm, summed, second, low, lo, part = run_forward(
        sizes, far_slots, slots,
        item_counts, lengths, vectors, inputs, cotangent, weight_in, weight_out, seq_table, hid_table,
        cid=2 * index + 2,
    )
    full, grad, small = run_backward(
        sizes, far_slots, slots, chunks // per_tick, chunk_rows * per_tick, parts,
        item_counts, lengths, vectors, part, act, dg, nrm, summed, second, low, weight_in, weight_out, seq_table, hid_table,
        cid=2 * index + 3,
    )
    return full, grad, small, lo


def per_device(
    inputs, item_counts, lengths, gain_one, shift_one, weight_in, bias_in, weight_out, bias_out, gain_two, shift_two, cotangent
):
    rows, slots, features = inputs.shape
    wide = weight_in.shape[1]
    sizes = (lax.axis_size("dp"), lax.axis_size("seq"))
    seq_total = rows * sizes[1]
    chunks = wide // WIDE
    chunk_rows = 2 * features * WIDE // LANES
    shape = jax.ShapeDtypeStruct

    seq_cos, seq_sin = dft_tables(seq_total)
    hid_cos, hid_sin = dft_tables(features)
    seq_table = [table.reshape(sizes[1], rows, seq_total) for table in (seq_cos, seq_sin)]
    seq_table = jnp.asarray(np.concatenate(seq_table, axis=1).astype(jnp.bfloat16))
    hid_table = jnp.asarray(np.concatenate([hid_cos, -hid_sin], axis=0).astype(jnp.bfloat16))
    vectors = jnp.concatenate([gain_one, shift_one, bias_out, gain_two, shift_two, bias_in]).reshape(-1, features)
    operands = (inputs, item_counts, lengths, vectors, weight_in, weight_out, cotangent, seq_table, hid_table)

    full, grad, small, lo = layer(slots, 0, sizes, *operands)

    side = 2 if chunks % 2 == 0 else 1
    wi_grad, wo_grad = pl.pallas_call(
        widen_kernel,
        name="widen",
        grid=(chunks // side,),
        out_shape=(shape((features, wide), F32), shape((wide, features), F32)),
        in_specs=[pl.BlockSpec((side, chunk_rows, LANES), lambda n: (n, 0, 0))],
        out_specs=(
            pl.BlockSpec((features, side * WIDE), lambda n: (0, n)),
            pl.BlockSpec((side * WIDE, features), lambda n: (n, 0)),
        ),
        compiler_params=pltpu.CompilerParams(vmem_limit_bytes=50 << 20),
    )(full.reshape(chunks, chunk_rows, LANES))

    step = rows // 2
    lo, grad = lo.reshape(slots, rows, features), grad.reshape(slots, rows, features)
    layer_out, input_grad = pl.pallas_call(
        functools.partial(restore_kernel, slots),
        name="restore",
        grid=(rows // step,),
        out_shape=(shape(inputs.shape, F32), shape(inputs.shape, F32)),
        in_specs=[SMEM] * 2 + [pl.BlockSpec((slots, step, features), lambda n: (0, n, 0))] * 2,
        out_specs=[pl.BlockSpec((step, slots, features), lambda n: (n, 0, 0))] * 2,
        scratch_shapes=[pltpu.SMEM((slots,), jnp.int32), pltpu.SMEM((slots,), jnp.int32)],
        compiler_params=pltpu.CompilerParams(vmem_limit_bytes=50 << 20),
    )(item_counts, lengths, lo, grad)

    small = small.reshape(-1)
    cuts = np.cumsum([features, features, wide, features, features, features])
    parts = [small[end - size : end] for end, size in zip(cuts, np.diff(cuts, prepend=0))]
    gain_one_grad, shift_one_grad, bias_in_grad, bias_out_grad, gain_two_grad, shift_two_grad = parts
    return (
        layer_out, input_grad, gain_one_grad, shift_one_grad, wi_grad, bias_in_grad, wo_grad, bias_out_grad, gain_two_grad, shift_two_grad,
    )


def solution(mesh):
    placed = (
        P("seq", "dp", None), P("dp"), P("dp"), P(), P(), P(), P(), P(), P(), P(), P(), P("seq", "dp", None),
    )
    wide = P("seq", "dp", None)
    return jax.shard_map(
        per_device,
        mesh=mesh,
        in_specs=placed,
        out_specs=(wide, wide, P(), P(), P(), P(), P(), P(), P(), P()),
        check_vma=False,
    )
```

time: 234 us -> 205 us (0.88)
  Pallas kernels: 224 us -> 195 us
    pallas_call x3, Pallas kernels: 215 us -> 189 us  [the longest x1 126 us: run_backward(): pl.pallas_call(functools.partial(backward_kernel, (sizes, far_slots, slot...]
    reshape x5 -> x1, local copies, waits for them, and re-layouts: 6.33 us -> 0.63 us  [per_device(): jnp.concatenate([gain_one, shift_one, bias_out, gain_two, shift_two, bias...]
    unnamed x2 -> x11, local copies, waits for them, and re-layouts: 0.01 us -> 5.35 us
    pallas_call x1, Pallas kernels: 8.82 us -> 5.3 us  [per_device(): pl.pallas_call(functools.partial(restore_kernel, slots), name='restore',...]
where the time goes in v3:
time: 205 us; the launch traced here: 204 us
  Pallas kernels  195 us (95%)
  local copies, waits for them, and re-layouts  7.91 us (4%)
    pallas_call x1, Pallas kernels, run_backward(): pl.pallas_call(functools.partial(backward_kernel, (sizes, far_slots, slot...  126 us
    pallas_call x1, Pallas kernels, run_forward(): pl.pallas_call(functools.partial(forward_kernel, (sizes, far_slots, slots...  53.4 us
    pallas_call x1, Pallas kernels, per_device(): pl.pallas_call(widen_kernel, name='widen', grid=(chunks // side,), out_sh...  9.76 us
    unnamed x11, local copies, waits for them, and re-layouts  5.35 us
    pallas_call x1, Pallas kernels, per_device(): pl.pallas_call(functools.partial(restore_kernel, slots), name='restore',...  5.3 us

profile of v3, /device:TPU:0, one launch (start us, length us, event | category | flops | bytes accessed | tf_op | source)
XLA Modules:
  0.0 204.0 jit_solution(697576030213660062)
XLA Ops:
  1.3 0.7 constant_dynamic-update-slice_fusion.5
  2.0 0.7 constant_dynamic-update-slice_fusion.4
  2.7 0.7 constant_dynamic-update-slice_fusion.3
  3.4 0.7 constant_dynamic-update-slice_fusion.2
  4.1 0.7 constant_dynamic-update-slice_fusion.1
  4.8 0.7 constant_dynamic-update-slice_fusion
  5.5 0.6 reshape.36.refs_2_
  6.1 53.4 %forward.1 = (bf16[6,1024,512]{2,1,0:T(8,128)(2,1)}, bf16[6,1024,512]{2,1,0:T(8,128)(2,1)}, bf16[1024,768]{1,0:T(8,128)(2,1)}, f32[1024,768]{1,0:T(8,128)}, f32[...) custom-call(s32[1]{0:T(128)S(6)} %copy.30.refs_0_.count_ref, ...), custom_call_target="tpu_custom_call" | custom-call | tf_op jit(solution)/shard_map/forward/pallas_call | solution.py:731
  59.5 0.0 copy-start.1
  59.5 126.3 %backward.1 = (bf16[6,6144,128]{2,1,0:T(8,128)(2,1)}, f32[1024,768]{1,0:T(8,128)}, f32[64,128]{1,0:T(8,128)}) custom-call(s32[1]{0:T(128)S(6)} %copy.30.refs_0_.count_ref, s32[8]{0:T(128)} %length_ref.1, f32[9,768]{1,0:T(8,128)} %reshape.36.refs_2_, f32[24,768]{1,0:T(8,128)} %get-tuple-element.26.refs_3_, bf16[6,1024,512]{2,1,0:T(8,128)(2,1)} %get-tuple-element.27.refs_4_, ...), custom_call_target="tpu_custom_call" | custom-call | tf_op jit(solution)/shard_map/backward/pallas_call | solution.py:789
  185.8 0.0 copy-done.1
  185.8 0.0 copy-start
  185.8 1.9 copy-done
  187.7 0.0 copy-start.2
  187.7 5.3 %restore.1 = (f32[128,8,768]{2,1,0:T(8,128)}, f32[128,8,768]{2,1,0:T(8,128)}) custom-call(s32[1]{0:T(128)S(6)} %copy.30.refs_0_.count_ref, s32[8]{0:T(128)S(1)} %copy-done.1, f32[8,128,768]{2,1,0:T(8,128)S(1)} %bitcast.14, f32[8,128,768]{2,1,0:T(8,128)} %bitcast.15), custom_call_target="tpu_custom_call" | custom-call | tf_op jit(solution)/shard_map/restore/pallas_call | solution.py:910
  193.0 0.0 copy-done.2
  193.0 0.6 slice_bitcast_fusion
  193.6 0.6 slice_bitcast_fusion.1
  194.2 9.8 %widen.1 = (f32[768,3072]{1,0:T(8,128)}, f32[3072,768]{1,0:T(8,128)}) custom-call(bf16[6,6144,128]{2,1,0:T(8,128)(2,1)} %get-tuple-element.37.full_ref), custom_call_target="tpu_custom_call" | custom-call | tf_op jit(solution)/shard_map/widen/pallas_call | solution.py:895
  (1 shorter events, 0.0 us)
Async XLA Ops:
  59.5 126.3 %copy-start.1 = (s32[8]{0:T(128)S(1)}, s32[8]{0:T(128)}, u32[]{:S(2)}) copy-start(s32[8]{0:T(128)} %length_ref.1) | copy-start | bytes 100
  185.8 1.9 copy-start
  187.7 5.3 %copy-start.2 = (f32[64,128]{1,0:T(8,128)S(1)}, f32[64,128]{1,0:T(8,128)}, u32[]{:S(2)}) copy-start(f32[64,128]{1,0:T(8,128)} %get-tuple-element.36) | copy-start | bytes 98308

commit v4 on v3

--- a/solution.py
+++ b/solution.py
@@ -191,10 +191,11 @@
 
 def forward_kernel(cfg, *refs):
     sizes, far_slots, slots, group = cfg
+    vec_refs, refs = refs[2:8], refs[:2] + refs[8:]
     (
-        count_ref, length_ref, vec_ref, x_hbm, cot_hbm, wi_hbm, wo_hbm, sc_hbm, hc_hbm,
+        count_ref, length_ref, x_hbm, cot_hbm, wi_hbm, wo_hbm, sc_hbm, hc_hbm,
         act_o, dg_o, nrm_o, sum_o, gs_o, gb_o, lo_o, part_o,
-        perm_s, slen_s, x_v, cot_v, wi_v, wo_v, sc_v, hc_v, buf, uv, sum_v, nrm_v, act_v, dg_v, gs_v, gb_v, lo_v, br_v,
+        perm_s, slen_s, x_v, cot_v, wi_v, wo_v, sc_v, hc_v, buf, uv, sum_v, nrm_v, act_v, dg_v, gs_v, gb_v, lo_v, br_v, vec_ref,
         load_sem, out_sem, send_sem, recv_sem,
     ) = refs
     rows, _, features = x_v.shape
@@ -214,6 +215,11 @@
         pltpu.make_async_copy(cot_hbm, cot_v, load_sem.at[5]),
     ]
     loads[0].start()
+    row = 0
+    for vec in vec_refs:
+        for i in range(vec.shape[0] // features):
+            vec_ref[row : row + 1, :] = vec[pl.ds(i * features, features)].reshape(1, features)
+            row += 1
     rank_slots(count_ref, length_ref, perm_s, slen_s, slots)
     greet([(exchange.dp, flipped(q, k)) for k in exchange.order])
     loads[0].wait()
@@ -353,17 +359,17 @@
     cube = Cube(sizes, mids)
     S = cube.stages
     (
-        count_ref, length_ref, vec_ref, part_ref,
+        count_ref, length_ref, gain_ref, part_ref,
         act_hbm, dg_hbm, nrm_hbm, sum_hbm, gs_hbm, gb_hbm, wi_hbm, wo_hbm, sc_hbm, hc_hbm,
         full_o, ig_o, small_o,
         perm_s, slen_s, gs_v, sum_v, nrm_v, gb_v, gh_v, gn_v, act_v, dg_v, wi_v, wo_v, sc_v, hc_v, buf, uv, ig_v,
-        bin_v, one_v, small_v, part_v, full,
-    ) = refs[:39]
-    landed = refs[39 : 39 + S]
+        bin_v, one_v, small_v, gain_v, part_v, full,
+    ) = refs[:40]
+    landed = refs[40 : 40 + S]
     (
         small_recv, load_sem, sum_sem, stream_sem, out_sem, ig_sem, send_sem, recv_sem,
         rs_s, rs_r, ag_s, ag_r, sm_s, sm_r,
-    ) = refs[39 + S :]
+    ) = refs[40 + S :]
     ticks, tick_rows, _ = part_v.shape
     message = tick_rows // parts
     chunks = act_hbm.shape[0]
@@ -480,6 +486,7 @@
 
     bin_v[...] = jnp.zeros_like(bin_v)
     one_v[...] = jnp.zeros_like(one_v)
+    gain_v[...] = gain_ref[...].reshape(1, features)
     gn_v[...] = jnp.zeros_like(gn_v)
     small_v[...] = jnp.zeros_like(small_v)
     loads[0].wait()
@@ -545,7 +552,7 @@
         grad = gn_v[here, :]
         one_v[0:8, :] = one_v[0:8, :] + fold8(grad * hat)
         one_v[8:16, :] = one_v[8:16, :] + fold8(grad)
-        grad = gs_v[here, :] + norm_back(grad * vec_ref[0:1, :], hat, inverse)
+        grad = gs_v[here, :] + norm_back(grad * gain_v[...], hat, inverse)
         gs_v[here, :] = grad
         buf[slot, pl.ds(aligned(first, rows), rows), :] = grad.astype(BF16)
         pl.when(i < far_slots)(lambda: exchange.start_own(slot, True))
@@ -692,23 +699,28 @@
     sends_done()
 
 
-def widen_kernel(full_ref, wi_ref, wo_ref):
+def output_kernel(slots, cuts, places, count_ref, length_ref, full_ref, lo_ref, ig_ref, small_ref, *refs):
+    wi_ref, wo_ref, lo_out, ig_out = refs[:4]
+    vector_refs, (perm_s, slen_s) = refs[4:-2], refs[-2:]
+    step = pl.program_id(0)
     features = wi_ref.shape[0]
-    for u in range(full_ref.shape[0]):
-        for i in range(features // LANES):
-            place = slice(u * WIDE, (u + 1) * WIDE)
-            wo_ref[place, i * LANES : (i + 1) * LANES] = full_ref[u, pl.ds(i * WIDE, WIDE), :].astype(F32)
-        for i in range(WIDE // LANES):
-            start = features // LANES * WIDE + i * features
-            place = slice(u * WIDE + i * LANES, u * WIDE + (i + 1) * LANES)
-            wi_ref[:, place] = full_ref[u, pl.ds(start, features), :].astype(F32)
-
-
-def restore_kernel(slots, count_ref, length_ref, lo_ref, ig_ref, lo_out, ig_out, perm_s, slen_s):
-    rank_slots(count_ref, length_ref, perm_s, slen_s, slots)
-    for j in range(slots):
-        lo_out[:, perm_s[j], :] = lo_ref[j]
-        ig_out[:, perm_s[j], :] = ig_ref[j]
+    for i in range(features // LANES):
+        wo_ref[:, i * LANES : (i + 1) * LANES] = full_ref[0, pl.ds(i * WIDE, WIDE), :].astype(F32)
+    for i in range(WIDE // LANES):
+        start = features // LANES * WIDE + i * features
+        wi_ref[:, i * LANES : (i + 1) * LANES] = full_ref[0, pl.ds(start, features), :].astype(F32)
+
+    @pl.when(step == 0)
+    def _():
+        rank_slots(count_ref, length_ref, perm_s, slen_s, slots)
+        for ref, start in zip(vector_refs, cuts):
+            ref[...] = small_ref[start : start + ref.shape[0], :]
+
+    @pl.when(step < places)
+    def _():
+        for j in range(slots):
+            lo_out[:, perm_s[j], :] = lo_ref[j]
+            ig_out[:, perm_s[j], :] = ig_ref[j]
 
 
 ANY = pl.BlockSpec(memory_space=pl.ANY)
@@ -723,8 +735,8 @@
 
 
 def run_forward(sizes, far_slots, slots, *operands, group=2, name="forward", cid=1):
-    rows, _, features = operands[3].shape
-    wide = operands[5].shape[1]
+    rows, _, features = operands[8].shape
+    wide = operands[10].shape[1]
     seq_total = rows * sizes[1]
     flat, batch, chunks = rows * slots, group * rows, wide // WIDE
     shape = jax.ShapeDtypeStruct
@@ -741,7 +753,7 @@
             shape((flat, features), F32),
             shape((24, features), F32),
         ),
-        in_specs=[SMEM] * 2 + [VMEM] + [ANY] * 6,
+        in_specs=[SMEM] * 2 + [VMEM] * 6 + [ANY] * 6,
         out_specs=[ANY] * 7 + [VMEM],
         scratch_shapes=[
             pltpu.SMEM((slots,), jnp.int32),
@@ -762,6 +774,7 @@
             pltpu.VMEM((flat, features), BF16),
             pltpu.VMEM((flat, features), F32),
             pltpu.VMEM((batch, features), F32),
+            pltpu.VMEM((5 + wide // features, features), F32),
             DMA((6,)),
             DMA((7,)),
             DMA((slots, sizes[1])),
@@ -817,6 +830,7 @@
             pltpu.VMEM((chunks, 8, WIDE), F32),
             pltpu.VMEM((16, features), F32),
             pltpu.VMEM((stages, 64, LANES), F32),
+            pltpu.VMEM((1, features), F32),
             pltpu.VMEM((ticks, tick_rows, LANES), BF16),
             pltpu.VMEM((ticks, tick_rows, LANES), BF16),
         ]
@@ -841,6 +855,40 @@
     )(*operands)
 
 
+def agree_kernel(groups, choices, span, count_ref, length_ref, choice_o, mine, theirs, send_sem, recv_sem):
+    dp, q = lax.axis_index("dp"), lax.axis_index("seq")
+
+    def peer(i):
+        return lax.rem(dp + i, groups)
+
+    def copy(i):
+        return pltpu.make_async_remote_copy(
+            src_ref=mine,
+            dst_ref=theirs.at[i],
+            send_sem=send_sem.at[i],
+            recv_sem=recv_sem.at[i],
+            device_id=(peer(i), q),
+            device_id_type=MESH,
+        )
+
+    greet([(peer(i), q) for i in range(1, groups)])
+    far = 0
+    for i in range(length_ref.shape[0]):
+        far = far + jnp.where((i < count_ref[0]) & (length_ref[i] > span), 1, 0)
+    need = jnp.full(mine.shape, far, jnp.int32)
+    mine[...] = need.astype(F32)
+    theirs[0] = need.astype(F32)
+    for i in range(1, groups):
+        copy(i).start()
+    for i in range(1, groups):
+        copy(i).wait()
+    most = jnp.max(theirs[...])
+    place = 0
+    for far in choices[:-1]:
+        place = place + jnp.where(most > far, 1, 0)
+    choice_o[0] = place
+
+
 def cut_messages(devices, chunks, chunk_rows):
     per_tick, parts = min(
         (count, -cut)
@@ -859,15 +907,48 @@
     per_tick, parts = cut_messages(sizes[0] * sizes[1], chunks, chunk_rows)
     act, dg, nrm, summed, second, low, lo, part = run_forward(
         sizes, far_slots, slots,
-        item_counts, lengths, vectors, inputs, cotangent, weight_in, weight_out, seq_table, hid_table,
+        item_counts, lengths, *vectors, inputs, cotangent, weight_in, weight_out, seq_table, hid_table,
         cid=2 * index + 2,
     )
     full, grad, small = run_backward(
         sizes, far_slots, slots, chunks // per_tick, chunk_rows * per_tick, parts,
-        item_counts, lengths, vectors, part, act, dg, nrm, summed, second, low, weight_in, weight_out, seq_table, hid_table,
+        item_counts, lengths, vectors[0], part, act, dg, nrm, summed, second, low, weight_in, weight_out, seq_table, hid_table,
         cid=2 * index + 3,
     )
-    return full, grad, small, lo
+    shape = jax.ShapeDtypeStruct
+    places = 1 << min(chunks.bit_length() - 1, 3)
+    step = rows // places
+    lo, grad = lo.reshape(slots, rows, features), grad.reshape(slots, rows, features)
+    heights = [size // LANES for size in (features, features, wide, features, features, features)]
+    cuts = [sum(heights[:i]) for i in range(len(heights))]
+    slot_first = pl.BlockSpec((slots, step, features), lambda n: (0, jnp.minimum(n, places - 1), 0))
+    place_first = pl.BlockSpec((step, slots, features), lambda n: (jnp.minimum(n, places - 1), 0, 0))
+    wi_grad, wo_grad, layer_out, input_grad, *vectors = pl.pallas_call(
+        functools.partial(output_kernel, slots, cuts, places),
+        name="output",
+        grid=(chunks,),
+        out_shape=(
+            shape((features, wide), F32),
+            shape((wide, features), F32),
+            shape(inputs.shape, F32),
+            shape(inputs.shape, F32),
+            *(shape((height, LANES), F32) for height in heights),
+        ),
+        in_specs=[SMEM] * 2 + [pl.BlockSpec((1, chunk_rows, LANES), lambda n: (n, 0, 0))] + [slot_first] * 2 + [VMEM],
+        out_specs=(
+            pl.BlockSpec((features, WIDE), lambda n: (0, n)),
+            pl.BlockSpec((WIDE, features), lambda n: (n, 0)),
+            place_first,
+            place_first,
+            *([VMEM] * len(heights)),
+        ),
+        scratch_shapes=[pltpu.SMEM((slots,), jnp.int32), pltpu.SMEM((slots,), jnp.int32)],
+        compiler_params=pltpu.CompilerParams(vmem_limit_bytes=60 << 20),
+    )(item_counts, lengths, full.reshape(chunks, chunk_rows, LANES), lo, grad, small)
+    gain_one_grad, shift_one_grad, bias_in_grad, bias_out_grad, gain_two_grad, shift_two_grad = [v.reshape(-1) for v in vectors]
+    return (
+        layer_out, input_grad, gain_one_grad, shift_one_grad, wi_grad, bias_in_grad, wo_grad, bias_out_grad, gain_two_grad, shift_two_grad,
+    )
 
 
 def per_device(
@@ -886,45 +967,27 @@
     seq_table = [table.reshape(sizes[1], rows, seq_total) for table in (seq_cos, seq_sin)]
     seq_table = jnp.asarray(np.concatenate(seq_table, axis=1).astype(jnp.bfloat16))
     hid_table = jnp.asarray(np.concatenate([hid_cos, -hid_sin], axis=0).astype(jnp.bfloat16))
-    vectors = jnp.concatenate([gain_one, shift_one, bias_out, gain_two, shift_two, bias_in]).reshape(-1, features)
+    vectors = (gain_one, shift_one, bias_out, gain_two, shift_two, bias_in)
     operands = (inputs, item_counts, lengths, vectors, weight_in, weight_out, cotangent, seq_table, hid_table)
 
-    full, grad, small, lo = layer(slots, 0, sizes, *operands)
-
-    side = 2 if chunks % 2 == 0 else 1
-    wi_grad, wo_grad = pl.pallas_call(
-        widen_kernel,
-        name="widen",
-        grid=(chunks // side,),
-        out_shape=(shape((features, wide), F32), shape((wide, features), F32)),
-        in_specs=[pl.BlockSpec((side, chunk_rows, LANES), lambda n: (n, 0, 0))],
-        out_specs=(
-            pl.BlockSpec((features, side * WIDE), lambda n: (0, n)),
-            pl.BlockSpec((side * WIDE, features), lambda n: (n, 0)),
-        ),
-        compiler_params=pltpu.CompilerParams(vmem_limit_bytes=50 << 20),
-    )(full.reshape(chunks, chunk_rows, LANES))
-
-    step = rows // 2
-    lo, grad = lo.reshape(slots, rows, features), grad.reshape(slots, rows, features)
-    layer_out, input_grad = pl.pallas_call(
-        functools.partial(restore_kernel, slots),
-        name="restore",
-        grid=(rows // step,),
-        out_shape=(shape(inputs.shape, F32), shape(inputs.shape, F32)),
-        in_specs=[SMEM] * 2 + [pl.BlockSpec((slots, step, features), lambda n: (0, n, 0))] * 2,
-        out_specs=[pl.BlockSpec((step, slots, features), lambda n: (n, 0, 0))] * 2,
-        scratch_shapes=[pltpu.SMEM((slots,), jnp.int32), pltpu.SMEM((slots,), jnp.int32)],
-        compiler_params=pltpu.CompilerParams(vmem_limit_bytes=50 << 20),
-    )(item_counts, lengths, lo, grad)
-
-    small = small.reshape(-1)
-    cuts = np.cumsum([features, features, wide, features, features, features])
-    parts = [small[end - size : end] for end, size in zip(cuts, np.diff(cuts, prepend=0))]
-    gain_one_grad, shift_one_grad, bias_in_grad, bias_out_grad, gain_two_grad, shift_two_grad = parts
-    return (
-        layer_out, input_grad, gain_one_grad, shift_one_grad, wi_grad, bias_in_grad, wo_grad, bias_out_grad, gain_two_grad, shift_two_grad,
-    )
+    choices = sorted({slots // 2, slots})
+    choice = pl.pallas_call(
+        functools.partial(agree_kernel, sizes[0], choices, 2 * rows),
+        name="agree",
+        out_shape=shape((1,), jnp.int32),
+        in_specs=[SMEM] * 2,
+        out_specs=SMEM,
+        scratch_shapes=[
+            pltpu.VMEM((8, LANES), F32),
+            pltpu.VMEM((sizes[0], 8, LANES), F32),
+            DMA((sizes[0],)),
+            DMA((sizes[0],)),
+        ],
+        compiler_params=pltpu.CompilerParams(collective_id=1, has_side_effects=True),
+    )(item_counts, lengths)
+    branches = [functools.partial(layer, far, index, sizes) for index, far in enumerate(choices)]
+
+    return lax.switch(choice[0], branches, *operands)
 
 
 def solution(mesh):

time: 205 us -> 175 us (0.85)
  Pallas kernels: 195 us -> 172 us
  local copies, waits for them, and re-layouts: 7.91 us -> 0.02 us
    pallas_call x1, Pallas kernels: 126 us -> 104 us  [run_backward(): pl.pallas_call(functools.partial(backward_kernel, (sizes, far_slots, slot...]
    pallas_call x1, Pallas kernels: 53.4 us -> 42.1 us  [run_forward(): pl.pallas_call(functools.partial(forward_kernel, (sizes, far_slots, slots...]
    pallas_call x2, Pallas kernels: 15.1 us -> 25.8 us  [the longest x1 16 us: layer(): pl.pallas_call(functools.partial(output_kernel, slots, cuts, places), nam...]
    unnamed x11 -> x0, local copies, waits for them, and re-layouts: 5.35 us -> none
where the time goes in v4:
time: 175 us; the launch traced here: 174 us
  Pallas kernels  172 us (98%)
  between operations  2.15 us (1%)
    pallas_call x1, Pallas kernels, run_backward(): pl.pallas_call(functools.partial(backward_kernel, (sizes, far_slots, slot...  104 us
    pallas_call x1, Pallas kernels, run_forward(): pl.pallas_call(functools.partial(forward_kernel, (sizes, far_slots, slots...  42.1 us
    pallas_call x1, Pallas kernels, layer(): pl.pallas_call(functools.partial(output_kernel, slots, cuts, places), nam...  16 us
    pallas_call x1, Pallas kernels, per_device(): pl.pallas_call(functools.partial(agree_kernel, sizes[0], choices, 2 * row...  9.82 us

profile of v4, /device:TPU:0, one launch (start us, length us, event | category | flops | bytes accessed | tf_op | source)
XLA Modules:
  0.0 174.3 jit_solution(3785778807792191436)
XLA Ops:
  1.3 9.8 %agree.1 = s32[1]{0:T(128)} custom-call(s32[1]{0:T(128)S(6)} %copy.44.count_ref, s32[8]{0:T(128)} %length_ref.1), custom_call_target="tpu_custom_call" | custom-call | tf_op jit(solution)/shard_map/agree/pallas_call | solution.py:974
  11.8 162.3 %conditional.1 = ((f32[768,3072]{1,0:T(8,128)}, f32[3072,768]{1,0:T(8,128)}, f32[128,8,768]{2,1,0:T(8,128)}, f32[128,8,768]{2,1,0:T(8,128)}, f32[6,128]{1,0:T(8,...) conditional(s32[]{:T(128)} %bitcast, (s32[1]{0:T(128)}, ...), branch_computations={%region_0.0_spmd.clone, %region_1.0_spmd.clone} | conditional | bytes 4206812 | solution.py:990
  11.8 0.0 copy-start
  11.8 0.0 copy-start.2
  11.8 0.0 copy-start.4
  11.9 42.1 %forward.2 = (bf16[6,1024,512]{2,1,0:T(8,128)(2,1)}, bf16[6,1024,512]{2,1,0:T(8,128)(2,1)}, bf16[1024,768]{1,0:T(8,128)(2,1)}, f32[1024,768]{1,0:T(8,128)}, f32[...) custom-call(s32[1]{0:T(128)} %get-tuple-element.148.refs_0_.count_ref, ...), custom_call_target="tpu_custom_call" | custom-call | tf_op jit(solution)/shard_map/cond/branch_0_fun/forward/pallas_call | solution.py:743
  54.0 0.0 copy-done
  54.0 0.0 copy-done.2
  54.0 0.0 copy-done.4
  54.0 103.9 %backward.2 = (bf16[6,6144,128]{2,1,0:T(8,128)(2,1)}, f32[1024,768]{1,0:T(8,128)}, f32[64,128]{1,0:T(8,128)}) custom-call(s32[1]{0:T(128)} %get-tuple-element.148.refs_0_.count_ref, s32[8]{0:T(128)S(1)} %copy-done.4, f32[768]{0:T(1024)S(1)} %copy-done.2, f32[24,768]{1,0:T(8,128)} %get-tuple-element.162.refs_3_, ...), custom_call_target="tpu_custom_call" | custom-call | tf_op jit(solution)/shard_map/cond/branch_0_fun/backward/pallas_call | solution.py:802
  157.9 16.0 %output.2 = (f32[768,3072]{1,0:T(8,128)}, f32[3072,768]{1,0:T(8,128)}, f32[128,8,768]{2,1,0:T(8,128)}, f32[128,8,768]{2,1,0:T(8,128)}, f32[6,128]{1,0:T(8,128)},...) custom-call(s32[1]{0:T(128)} %get-tuple-element.148.refs_0_.count_ref, ...), custom_call_target="tpu_custom_call" | custom-call | tf_op jit(solution)/shard_map/cond/branch_0_fun/output/pallas_call | solution.py:926
Async XLA Ops:
  11.8 42.2 %copy-start = (bf16[4,256,512]{2,1,0:T(8,128)(2,1)S(1)}, bf16[4,256,512]{2,1,0:T(8,128)(2,1)}, u32[]{:S(2)}) copy-start(bf16[4,256,512]{2,1,0:T(8,128)(2,1)} %get-tuple-element.160.refs_12_) | copy-start | bytes 3145732 | tf_op jit(solution)/shard_map/cond
  11.8 42.2 %copy-start.2 = (f32[768]{0:T(1024)S(1)}, f32[768]{0:T(1024)}, u32[]{:S(2)}) copy-start(f32[768]{0:T(1024)} %get-tuple-element.150.refs_2_) | copy-start | bytes 9220 | tf_op jit(solution)/shard_map/cond
  11.8 42.2 %copy-start.4 = (s32[8]{0:T(128)S(1)}, s32[8]{0:T(128)}, u32[]{:S(2)}) copy-start(s32[8]{0:T(128)} %get-tuple-element.149.refs_1_.length_ref) | copy-start | bytes 100 | tf_op jit(solution)/shard_map/cond

commit v5 on v4

--- a/solution.py
+++ b/solution.py
@@ -123,7 +123,7 @@
     barrier = pltpu.get_barrier_semaphore()
     for partner in partners:
         pl.semaphore_signal(barrier, inc=1, device_id=partner, device_id_type=MESH)
-    pl.semaphore_wait(barrier, len(partners))
+    return lambda: pl.semaphore_wait(barrier, len(partners))
 
 
 def rank_slots(count_ref, length_ref, perm_s, slen_s, slots):
@@ -193,7 +193,7 @@
     sizes, far_slots, slots, group = cfg
     vec_refs, refs = refs[2:8], refs[:2] + refs[8:]
     (
-        count_ref, length_ref, x_hbm, cot_hbm, wi_hbm, wo_hbm, sc_hbm, hc_hbm,
+        count_ref, length_ref, low_hbm, x_hbm, cot_hbm, wi_hbm, wo_hbm, sc_hbm, hc_hbm,
         act_o, dg_o, nrm_o, sum_o, gs_o, gb_o, lo_o, part_o,
         perm_s, slen_s, x_v, cot_v, wi_v, wo_v, sc_v, hc_v, buf, uv, sum_v, nrm_v, act_v, dg_v, gs_v, gb_v, lo_v, br_v, vec_ref,
         load_sem, out_sem, send_sem, recv_sem,
@@ -207,30 +207,31 @@
     first = q * rows
     gain_one, shift_one, bias_out, gain_two, shift_two = (lambda i=i: vec_ref[i : i + 1, :] for i in range(5))
     loads = [
-        pltpu.make_async_copy(x_hbm, x_v, load_sem.at[0]),
+        pltpu.make_async_copy(low_hbm, buf.at[:, pl.ds(aligned(first, rows), rows), :], load_sem.at[0]),
         pltpu.make_async_copy(sc_hbm.at[q], sc_v, load_sem.at[1]),
         pltpu.make_async_copy(hc_hbm, hc_v, load_sem.at[2]),
+        pltpu.make_async_copy(x_hbm, x_v, load_sem.at[6]),
         pltpu.make_async_copy(wi_hbm, wi_v, load_sem.at[3]),
         pltpu.make_async_copy(wo_hbm, wo_v, load_sem.at[4]),
         pltpu.make_async_copy(cot_hbm, cot_v, load_sem.at[5]),
     ]
     loads[0].start()
+    met = greet([(exchange.dp, flipped(q, k)) for k in exchange.order])
     row = 0
     for vec in vec_refs:
         for i in range(vec.shape[0] // features):
             vec_ref[row : row + 1, :] = vec[pl.ds(i * features, features)].reshape(1, features)
             row += 1
     rank_slots(count_ref, length_ref, perm_s, slen_s, slots)
-    greet([(exchange.dp, flipped(q, k)) for k in exchange.order])
+    for load in loads[1:3]:
+        load.start()
     loads[0].wait()
-    for load in loads[1:]:
+    for load in loads[3:5]:
         load.start()
+    met()
 
     def prepare(i, _):
         slot = jnp.where(i < far_slots, far_slots - 1 - i, i) if far_slots < slots else slots - 1 - i
-        value = jnp.where(live_rows(slen_s, slot, first, rows), x_v[:, perm_s[slot], :], 0.0)
-        sum_v[pl.ds(aligned(slot * rows, rows), rows), :] = value
-        buf[slot, pl.ds(aligned(first, rows), rows), :] = value.astype(BF16)
         pl.when(i < far_slots)(lambda: exchange.start_own(slot, True))
         if far_slots < slots:
             pl.when(i >= far_slots)(lambda: exchange.start_own(slot, False))
@@ -248,18 +249,20 @@
 
     def outs(base):
         place = pl.ds(base, batch)
-        copies = [
+        early = [
             pltpu.make_async_copy(nrm_v.at[place], nrm_o.at[place], out_sem.at[0]),
             pltpu.make_async_copy(sum_v.at[place], sum_o.at[place], out_sem.at[1]),
+        ]
+        for n in range(wide // WIDE):
+            cut = pl.ds(n * WIDE, WIDE)
+            early.append(pltpu.make_async_copy(act_v.at[place, cut], act_o.at[n, place], out_sem.at[4]))
+            early.append(pltpu.make_async_copy(dg_v.at[place, cut], dg_o.at[n, place], out_sem.at[5]))
+        late = [
             pltpu.make_async_copy(gs_v.at[place], gs_o.at[place], out_sem.at[2]),
             pltpu.make_async_copy(lo_v.at[place], lo_o.at[place], out_sem.at[3]),
             pltpu.make_async_copy(gb_v.at[place], gb_o.at[place], out_sem.at[6]),
         ]
-        for n in range(wide // WIDE):
-            cut = pl.ds(n * WIDE, WIDE)
-            copies.append(pltpu.make_async_copy(act_v.at[place, cut], act_o.at[n, place], out_sem.at[4]))
-            copies.append(pltpu.make_async_copy(dg_v.at[place, cut], dg_o.at[n, place], out_sem.at[5]))
-        return copies
+        return early, late
 
     def bring(slot0):
         for k in reversed(range(group)):
@@ -278,12 +281,16 @@
             pl.when(i >= near_groups)(lambda: mixing(slot0, True))
         if near_groups > 0:
             pl.when(i < near_groups)(lambda: mixing(slot0, False))
-        mixed = jnp.dot(uv[...], hc_v[...], preferred_element_type=F32)
-        sum_v[place, :] = sum_v[place, :] + (mixed * scale).astype(BF16).astype(F32)
+        br_v[...] = jnp.dot(uv[...], hc_v[...], preferred_element_type=F32)
+        pl.when(i == 0)(loads[3].wait)
 
         def norm_one(k, _):
             here = pl.ds(aligned(base + k * rows, rows), rows)
-            hat, _ = normalize(sum_v[here, :])
+            mixed = (br_v[pl.ds(aligned(k * rows, rows), rows), :] * scale).astype(BF16).astype(F32)
+            live = live_rows(slen_s, slot0 + k, first, rows)
+            total = jnp.where(live, x_v[:, perm_s[slot0 + k], :], 0.0) + mixed
+            sum_v[here, :] = total
+            hat, _ = normalize(total)
             nrm_v[here, :] = (hat * gain_one() + shift_one()).astype(BF16)
             return 0
 
@@ -291,8 +298,9 @@
 
         @pl.when(i == 0)
         def _():
-            for load in loads[3:]:
-                load.wait()
+            loads[4].wait()
+            for load in loads[5:]:
+                load.start()
 
         def expand(n, _):
             cut = pl.ds(aligned(n * span, span), span)
@@ -304,6 +312,15 @@
             return 0
 
         lax.fori_loop(0, wide // span, expand, 0)
+        for copy in outs(base)[0]:
+            copy.start()
+        if near_groups < count:
+
+            @pl.when((i + 1 >= near_groups) & (i + 1 < count))
+            def _():
+                bring(group_at(i + 1, near_groups, count) * group)
+
+        pl.when(i == 0)(loads[5].wait)
         br_v[...] = jnp.dot(act_v[place, :], wo_v[...], preferred_element_type=F32)
 
         def norm_two(k, _):
@@ -323,15 +340,10 @@
             part_o[16:24, :] = part_o[16:24, :] + fold8(low.astype(F32))
             return 0
 
+        pl.when(i == 0)(loads[6].wait)
         lax.fori_loop(0, group, norm_two, 0)
-        for copy in outs(base):
+        for copy in outs(base)[1]:
             copy.start()
-        if near_groups < count:
-
-            @pl.when((i + 1 >= near_groups) & (i + 1 < count))
-            def _():
-                bring(group_at(i + 1, near_groups, count) * group)
-
         return 0
 
     if near_groups == 0:
@@ -347,8 +359,9 @@
     lax.fori_loop(0, slots, finish, 0)
 
     def flush(g, _):
-        for copy in outs(aligned(g * batch, batch)):
-            copy.wait()
+        for copies in outs(aligned(g * batch, batch)):
+            for copy in copies:
+                copy.wait()
         return 0
 
     lax.fori_loop(0, count, flush, 0)
@@ -406,14 +419,9 @@
         ]
 
     loads[0].start()
-    for copy in streams(0, 0):
-        copy.start()
-    for load in loads[1:]:
-        load.start()
-    for i in range(2):
-        sum_copy(i).start()
+    streams(0, 0)[0].start()
+    met = greet([cube.partner(bit) for bit in cube.bits])
     rank_slots(count_ref, length_ref, perm_s, slen_s, slots)
-    greet([cube.partner(bit) for bit in cube.bits])
 
     starts = [[j * message + cube.offset(j, level, message) for level in range(S + 1)] for j in range(parts)]
 
@@ -490,6 +498,17 @@
     gn_v[...] = jnp.zeros_like(gn_v)
     small_v[...] = jnp.zeros_like(small_v)
     loads[0].wait()
+    for copy in streams(0, 0)[1:]:
+        copy.start()
+    loads[1].start()
+    met()
+
+    def load_rest():
+        for load in loads[2:]:
+            load.start()
+        for i in range(2):
+            sum_copy(i).start()
+
 
     def contract(left, right, dims):
         return lax.dot_general(left, right, ((dims, dims), ((), ())), preferred_element_type=F32)
@@ -672,6 +691,7 @@
     )
 
     def body(tick, _):
+        pl.when(tick == 1)(load_rest)
         for j in range(parts):
             pl.when(tick < ticks)(lambda: compute(tick, j))
             events(tick, j)
@@ -727,7 +747,7 @@
 SMEM = pl.BlockSpec(memory_space=pltpu.SMEM)
 VMEM = pl.BlockSpec(memory_space=pltpu.VMEM)
 DMA = pltpu.SemaphoreType.DMA
-LAGS = [4, 4, 4, 4, 4, 4, 4, 4, 4, 4]
+LAGS = [3, 5, 4, 3, 3, 3, 3, 4, 6, 3]
 PLAN = (4, 1, 4, 1)
 FAR_PLAN = (4, 1, 4, 1)
 MIDS = ((0, 1, 2), (1, 0, 2), (2, 0, 1), (1, 2, 0))
@@ -735,8 +755,8 @@
 
 
 def run_forward(sizes, far_slots, slots, *operands, group=2, name="forward", cid=1):
-    rows, _, features = operands[8].shape
-    wide = operands[10].shape[1]
+    rows, _, features = operands[9].shape
+    wide = operands[11].shape[1]
     seq_total = rows * sizes[1]
     flat, batch, chunks = rows * slots, group * rows, wide // WIDE
     shape = jax.ShapeDtypeStruct
@@ -753,7 +773,7 @@
             shape((flat, features), F32),
             shape((24, features), F32),
         ),
-        in_specs=[SMEM] * 2 + [VMEM] * 6 + [ANY] * 6,
+        in_specs=[SMEM] * 2 + [VMEM] * 6 + [ANY] * 7,
         out_specs=[ANY] * 7 + [VMEM],
         scratch_shapes=[
             pltpu.SMEM((slots,), jnp.int32),
@@ -775,7 +795,7 @@
             pltpu.VMEM((flat, features), F32),
             pltpu.VMEM((batch, features), F32),
             pltpu.VMEM((5 + wide // features, features), F32),
-            DMA((6,)),
+            DMA((7,)),
             DMA((7,)),
             DMA((slots, sizes[1])),
             DMA((slots, sizes[1])),
@@ -855,8 +875,13 @@
     )(*operands)
 
 
-def agree_kernel(groups, choices, span, count_ref, length_ref, choice_o, mine, theirs, send_sem, recv_sem):
+def agree_kernel(
+    groups, choices, span, count_ref, length_ref, x_hbm, choice_o, low_o, x_v, low_v, perm_s, slen_s, mine, theirs, load_sem, send_sem, recv_sem
+):
     dp, q = lax.axis_index("dp"), lax.axis_index("seq")
+    rows, slots, _ = x_v.shape
+    load = pltpu.make_async_copy(x_hbm, x_v, load_sem.at[0])
+    load.start()
 
     def peer(i):
         return lax.rem(dp + i, groups)
@@ -871,15 +896,27 @@
             device_id_type=MESH,
         )
 
-    greet([(peer(i), q) for i in range(1, groups)])
+    met = greet([(peer(i), q) for i in range(1, groups)])
     far = 0
     for i in range(length_ref.shape[0]):
         far = far + jnp.where((i < count_ref[0]) & (length_ref[i] > span), 1, 0)
     need = jnp.full(mine.shape, far, jnp.int32)
     mine[...] = need.astype(F32)
     theirs[0] = need.astype(F32)
+    met()
     for i in range(1, groups):
         copy(i).start()
+    rank_slots(count_ref, length_ref, perm_s, slen_s, slots)
+    load.wait()
+    store = pltpu.make_async_copy(low_v, low_o, load_sem.at[1])
+
+    def prepare(slot, _):
+        live = live_rows(slen_s, slot, q * rows, rows)
+        low_v[slot] = jnp.where(live, x_v[:, perm_s[slot], :], 0.0).astype(BF16)
+        return 0
+
+    lax.fori_loop(0, slots, prepare, 0)
+    store.start()
     for i in range(1, groups):
         copy(i).wait()
     most = jnp.max(theirs[...])
@@ -887,6 +924,7 @@
     for far in choices[:-1]:
         place = place + jnp.where(most > far, 1, 0)
     choice_o[0] = place
+    store.wait()
 
 
 def cut_messages(devices, chunks, chunk_rows):
@@ -899,7 +937,7 @@
     return per_tick, -parts
 
 
-def layer(far_slots, index, sizes, inputs, item_counts, lengths, vectors, weight_in, weight_out, cotangent, seq_table, hid_table):
+def layer(far_slots, index, sizes, low_input, inputs, item_counts, lengths, vectors, weight_in, weight_out, cotangent, seq_table, hid_table):
     rows, slots, features = inputs.shape
     wide = weight_in.shape[1]
     chunks = wide // WIDE
@@ -907,7 +945,7 @@
     per_tick, parts = cut_messages(sizes[0] * sizes[1], chunks, chunk_rows)
     act, dg, nrm, summed, second, low, lo, part = run_forward(
         sizes, far_slots, slots,
-        item_counts, lengths, *vectors, inputs, cotangent, weight_in, weight_out, seq_table, hid_table,
+        item_counts, lengths, *vectors, low_input, inputs, cotangent, weight_in, weight_out, seq_table, hid_table,
         cid=2 * index + 2,
     )
     full, grad, small = run_backward(
@@ -971,23 +1009,28 @@
     operands = (inputs, item_counts, lengths, vectors, weight_in, weight_out, cotangent, seq_table, hid_table)
 
     choices = sorted({slots // 2, slots})
-    choice = pl.pallas_call(
+    choice, low = pl.pallas_call(
         functools.partial(agree_kernel, sizes[0], choices, 2 * rows),
         name="agree",
-        out_shape=shape((1,), jnp.int32),
-        in_specs=[SMEM] * 2,
-        out_specs=SMEM,
+        out_shape=(shape((1,), jnp.int32), shape((slots, rows, features), BF16)),
+        in_specs=[SMEM] * 2 + [ANY],
+        out_specs=(SMEM, ANY),
         scratch_shapes=[
+            pltpu.VMEM(inputs.shape, F32),
+            pltpu.VMEM((slots, rows, features), BF16),
+            pltpu.SMEM((slots,), jnp.int32),
+            pltpu.SMEM((slots,), jnp.int32),
             pltpu.VMEM((8, LANES), F32),
             pltpu.VMEM((sizes[0], 8, LANES), F32),
+            DMA((2,)),
             DMA((sizes[0],)),
             DMA((sizes[0],)),
         ],
         compiler_params=pltpu.CompilerParams(collective_id=1, has_side_effects=True),
-    )(item_counts, lengths)
+    )(item_counts, lengths, inputs)
     branches = [functools.partial(layer, far, index, sizes) for index, far in enumerate(choices)]
 
-    return lax.switch(choice[0], branches, *operands)
+    return lax.switch(choice[0], branches, low, *operands)
 
 
 def solution(mesh):

time: 175 us -> 170 us (0.971)
  Pallas kernels: 172 us -> 166 us
    pallas_call x1, Pallas kernels: 42.1 us -> 37.2 us  [run_forward(): pl.pallas_call(functools.partial(forward_kernel, (sizes, far_slots, slots...]
where the time goes in v5:
time: 170 us; the launch traced here: 169 us
  Pallas kernels  166 us (98%)
  between operations  2.24 us (1%)
    pallas_call x1, Pallas kernels, run_backward(): pl.pallas_call(functools.partial(backward_kernel, (sizes, far_slots, slot...  103 us
    pallas_call x1, Pallas kernels, run_forward(): pl.pallas_call(functools.partial(forward_kernel, (sizes, far_slots, slots...  37.2 us
    pallas_call x1, Pallas kernels, layer(): pl.pallas_call(functools.partial(output_kernel, slots, cuts, places), nam...  16 us
    pallas_call x1, Pallas kernels, per_device(): pl.pallas_call(functools.partial(agree_kernel, sizes[0], choices, 2 * row...  9.84 us

profile of v5, /device:TPU:0, one launch (start us, length us, event | category | flops | bytes accessed | tf_op | source)
XLA Modules:
  0.0 168.6 jit_solution(7405420969135610929)
XLA Ops:
  0.6 0.0 copy-start
  0.7 0.0 copy-start.3
  0.7 0.0 copy-start.7
  0.7 0.0 copy-start.6
  0.7 0.0 copy-start.5
  0.7 0.0 copy-start.2
  0.7 0.0 copy-start.4
  0.7 0.0 copy-start.1
  1.4 9.8 %agree.1 = (s32[1]{0:T(128)}, bf16[8,128,768]{2,1,0:T(8,128)(2,1)}) custom-call(s32[1]{0:T(128)S(6)} %copy.44.count_ref, s32[8]{0:T(128)} %length_ref.1, f32[128,8,768]{2,1,0:T(8,128)} %x_hbm.1), custom_call_target="tpu_custom_call" | custom-call | tf_op jit(solution)/shard_map/agree/pallas_call | solution.py:1012
  11.9 0.0 copy-done
  11.9 0.0 copy-done.3
  11.9 0.0 copy-done.7
  11.9 0.0 copy-done.6
  11.9 0.0 copy-done.5
  11.9 0.0 copy-done.2
  11.9 0.0 copy-done.4
  11.9 0.0 copy-done.1
  12.0 156.5 %conditional.1 = ((f32[768,3072]{1,0:T(8,128)}, f32[3072,768]{1,0:T(8,128)}, f32[128,8,768]{2,1,0:T(8,128)}, f32[128,8,768]{2,1,0:T(8,128)}, f32[6,128]{1,0:T(8,...) conditional(s32[]{:T(128)} %bitcast, (s32[1]{0:T(128)}, ...), branch_computations={%region_0.0_spmd.clone, %region_1.0_spmd.clone} | conditional | bytes 8 | solution.py:1033
  12.0 37.2 %forward.2 = (bf16[6,1024,512]{2,1,0:T(8,128)(2,1)}, bf16[6,1024,512]{2,1,0:T(8,128)(2,1)}, bf16[1024,768]{1,0:T(8,128)(2,1)}, f32[1024,768]{1,0:T(8,128)}, f32[...) custom-call(s32[1]{0:T(128)} %get-tuple-element.158.refs_0_.count_ref, ...), custom_call_target="tpu_custom_call" | custom-call | tf_op jit(solution)/shard_map/cond/branch_0_fun/forward/pallas_call | solution.py:763
  49.2 103.1 %backward.2 = (bf16[6,6144,128]{2,1,0:T(8,128)(2,1)}, f32[1024,768]{1,0:T(8,128)}, f32[64,128]{1,0:T(8,128)}) custom-call(s32[1]{0:T(128)} %get-tuple-element.158.refs_0_.count_ref, s32[8]{0:T(128)S(1)} %get-tuple-element.159.refs_1_.length_ref, f32[768]{0:T(1024)S(1)} %get-tuple-element.160.refs_2_, f32[24,768]{1,0:T(8,128)} %get-tuple-element.173.refs_3_, ...), custom_call_target="tpu_custom_call" | custom-call | tf_op jit(solution)/shard_map/cond/branch_0_fun/backward/pallas_call | solution.py:822
  152.3 16.0 %output.2 = (f32[768,3072]{1,0:T(8,128)}, f32[3072,768]{1,0:T(8,128)}, f32[128,8,768]{2,1,0:T(8,128)}, f32[128,8,768]{2,1,0:T(8,128)}, f32[6,128]{1,0:T(8,128)},...) custom-call(s32[1]{0:T(128)} %get-tuple-element.158.refs_0_.count_ref, ...), custom_call_target="tpu_custom_call" | custom-call | tf_op jit(solution)/shard_map/cond/branch_0_fun/output/pallas_call | solution.py:964
Async XLA Ops:
  0.6 11.2 %copy-start = (bf16[4,256,512]{2,1,0:T(8,128)(2,1)S(1)}, bf16[4,256,512]{2,1,0:T(8,128)(2,1)}, u32[]{:S(2)}) copy-start(bf16[4,256,512]{2,1,0:T(8,128)(2,1)} %constant.10.clone) | copy-start | bytes 3145732
  0.7 11.2 %copy-start.3 = (s32[8]{0:T(128)S(1)}, s32[8]{0:T(128)}, u32[]{:S(2)}) copy-start(s32[8]{0:T(128)} %length_ref.1) | copy-start | bytes 100
  0.7 11.2 %copy-start.7 = (f32[768]{0:T(1024)S(1)}, f32[768]{0:T(1024)}, u32[]{:S(2)}) copy-start(f32[768]{0:T(1024)} %param.26) | copy-start | bytes 9220
  0.7 11.2 %copy-start.6 = (f32[768]{0:T(1024)S(1)}, f32[768]{0:T(1024)}, u32[]{:S(2)}) copy-start(f32[768]{0:T(1024)} %param.25) | copy-start | bytes 9220
  0.7 11.2 %copy-start.5 = (f32[768]{0:T(1024)S(1)}, f32[768]{0:T(1024)}, u32[]{:S(2)}) copy-start(f32[768]{0:T(1024)} %param.24) | copy-start | bytes 9220
  0.7 11.2 %copy-start.2 = (f32[3072]{0:T(1024)S(1)}, f32[3072]{0:T(1024)}, u32[]{:S(2)}) copy-start(f32[3072]{0:T(1024)} %param.22) | copy-start | bytes 36868
  0.7 11.2 %copy-start.4 = (f32[768]{0:T(1024)S(1)}, f32[768]{0:T(1024)}, u32[]{:S(2)}) copy-start(f32[768]{0:T(1024)} %param.20) | copy-start | bytes 9220
  0.7 11.2 %copy-start.1 = (f32[768]{0:T(1024)S(1)}, f32[768]{0:T(1024)}, u32[]{:S(2)}) copy-start(f32[768]{0:T(1024)} %param.19) | copy-start | bytes 9220
